TPU v7x, 256 devices: a whole 4x4x8 slice. The times are simulated.
256 devices in a mesh: ctx: 32 (over z, x_lo, core), head: 8 (over y, x_hi).
Axes of the slice: x: 4 (x_hi: 2, x_lo: 2; x = x_hi * 2 + x_lo), y: 4, z: 8, core: 2. Of those that a mesh axis runs over, the one named last changes fastest.
Arguments:
- vid_query: bfloat16 [32, 8192, 128], P('head', 'ctx')
- vid_key: bfloat16 [32, 8192, 128], P('head', 'ctx')
- vid_value: bfloat16 [32, 8192, 128], P('head', 'ctx'), may hold values from -6 to 6
- vid_out: bfloat16 [32, 8192, 128], P('head', 'ctx'), may hold values from -6 to 6
- vid_grad: bfloat16 [32, 8192, 128], P('head', 'ctx'), may hold values from -96 to 96
- vid_lse: float32 [32, 8192], P('head', 'ctx'), as said below
- vid_mask: int32 [32, 8192, 256], P('head', 'ctx'), may hold values from 0 to 255
- aud_query: bfloat16 [32, 2048, 128], P('head', 'ctx')
- aud_key: bfloat16 [32, 2048, 128], P('head', 'ctx')
- aud_value: bfloat16 [32, 2048, 128], P('head', 'ctx'), may hold values from -6 to 6
- aud_out: bfloat16 [32, 2048, 128], P('head', 'ctx'), may hold values from -6 to 6
- aud_grad: bfloat16 [32, 2048, 128], P('head', 'ctx'), may hold values from -384 to 384
- aud_lse: float32 [32, 2048], P('head', 'ctx'), as said below
- aud_mask: int32 [32, 2048, 1024], P('head', None, 'ctx'), may hold values from 0 to 255
- gain_vq: float32 [32, 128], P('head'), may hold values from 0.5 to 1.5
- gain_ak: float32 [32, 128], P('head'), may hold values from 0.5 to 1.5
- gain_aq: float32 [32, 128], P('head'), may hold values from 0.5 to 1.5
- gain_vk: float32 [32, 128], P('head'), may hold values from 0.5 to 1.5
Outputs:
- grad_vid_query: bfloat16 [32, 8192, 128], P('head', 'ctx')
- grad_vid_key: bfloat16 [32, 8192, 128], P('head', 'ctx')
- grad_vid_value: bfloat16 [32, 8192, 128], P('head', 'ctx')
- grad_aud_query: bfloat16 [32, 2048, 128], P('head', 'ctx')
- grad_aud_key: bfloat16 [32, 2048, 128], P('head', 'ctx')
- grad_aud_value: bfloat16 [32, 2048, 128], P('head', 'ctx')
Inputs may be any that keep to these rules, and one draw needn't show every extreme that they name: `vid_lse`: every entry lies between ln(2048) and ln(2048) + 1.5. `aud_lse`: every entry lies between ln(8192) and ln(8192) + 1.5.
All inputs are finite; a program needn't handle non-finite values.
Results may differ from a plain program's by a relative error of at most 0.011.
Values may be sent and summed in bfloat16 or wider, within the bound.
No kernel may reach another device: no remote copies, remote signals or barrier semaphores. Data moves between devices by JAX's collectives and lax.ppermute only.
A program may use at most 128 MiB of HBM per device.

v0:
```python
import math

import jax
import jax.numpy as jnp
from jax import lax
from jax.sharding import PartitionSpec as P

EPS = 1e-06


def unpack_bits(word_rows):
    shifts = jnp.arange(8, dtype=jnp.int32)
    bit_values = jnp.bitwise_and(jnp.right_shift(word_rows[..., None], shifts), 1)
    return bit_values.reshape(word_rows.shape[:-1] + (word_rows.shape[-1] * 8,)).astype(jnp.float32)


def dot_rows(left, right):
    return lax.dot_general(
        left, right, (((2,), (2,)), ((0,), (0,))), preferred_element_type=jnp.float32
    )


def dot_cols(left, right):
    return lax.dot_general(
        left, right, (((1,), (1,)), ((0,), (0,))), preferred_element_type=jnp.float32
    )


def dot_plain(left, right):
    return lax.dot_general(
        left, right, (((2,), (1,)), ((0,), (0,))), preferred_element_type=jnp.float32
    )


def add_rows(buffer, update, offset):
    current = lax.dynamic_slice_in_dim(buffer, offset, update.shape[1], 1)
    return lax.dynamic_update_slice_in_dim(buffer, current + update, offset, 1)


def square_sums(tokens):
    values = tokens.astype(jnp.float32)
    return jnp.sum(values * values, axis=(0, 2))


def normalize(tokens, scales, gain_rows):
    return (tokens.astype(jnp.float32) * scales[None, :, None] * gain_rows[:, None, :]).astype(
        jnp.bfloat16
    )


def norm_parts(tokens, scales, gain_rows, upstream):
    weighted = upstream * gain_rows[:, None, :]
    unit_rows = tokens.astype(jnp.float32) * scales[None, :, None]
    return (weighted, unit_rows, jnp.sum(weighted * unit_rows, axis=(0, 2)))


def norm_finish(weighted, unit_rows, scales, product, feature_count):
    mean_term = product / feature_count
    return (scales[None, :, None] * (weighted - unit_rows * mean_term[None, :, None])).astype(
        jnp.bfloat16
    )


def block_terms(
    query_rows, key_rows, value_rows, upstream, lse_rows, delta_rows, word_rows, score_scale
):
    scores = dot_rows(query_rows, key_rows) * score_scale
    attention = jnp.exp(scores - lse_rows[:, :, None])
    kept_mask = unpack_bits(word_rows)
    dropped = (2.0 * kept_mask * attention).astype(jnp.bfloat16)
    prob_grad = 2.0 * kept_mask * dot_rows(upstream, value_rows)
    score_grad = (attention * (prob_grad - delta_rows[:, :, None])).astype(jnp.bfloat16)
    return (dropped, score_grad)


def local(
    vid_query,
    vid_key,
    vid_value,
    vid_out,
    vid_grad,
    vid_lse,
    vid_mask,
    aud_query,
    aud_key,
    aud_value,
    aud_out,
    aud_grad,
    aud_lse,
    aud_mask,
    gain_vq,
    gain_ak,
    gain_aq,
    gain_vk,
):
    head_count = vid_query.shape[0]
    head_dim = vid_query.shape[2]
    feature_count = lax.axis_size("head") * head_count * head_dim
    score_scale = head_dim ** (-0.5)
    total_vq, total_ak, total_aq, total_vk = lax.psum(
        (
            square_sums(vid_query),
            square_sums(aud_key),
            square_sums(aud_query),
            square_sums(vid_key),
        ),
        "head",
    )
    scale_vq = lax.rsqrt(total_vq / feature_count + EPS)
    scale_ak = lax.rsqrt(total_ak / feature_count + EPS)
    scale_aq = lax.rsqrt(total_aq / feature_count + EPS)
    scale_vk = lax.rsqrt(total_vk / feature_count + EPS)
    normed_vq = normalize(vid_query, scale_vq, gain_vq)
    normed_ak = normalize(aud_key, scale_ak, gain_ak)
    normed_aq = normalize(aud_query, scale_aq, gain_aq)
    normed_vk = normalize(vid_key, scale_vk, gain_vk)
    video_delta = jnp.sum(vid_grad.astype(jnp.float32) * vid_out.astype(jnp.float32), axis=2)
    audio_delta = jnp.sum(aud_grad.astype(jnp.float32) * aud_out.astype(jnp.float32), axis=2)
    lse_whole, delta_whole = (
        lax.all_gather(aud_lse, "ctx", axis=1, tiled=True),
        lax.all_gather(audio_delta, "ctx", axis=1, tiled=True),
    )
    audio_total = lse_whole.shape[1]
    local_video = vid_value.shape[1]

    def video_side(key_rows, value_rows, offset):
        word_rows = lax.dynamic_slice_in_dim(vid_mask, offset // 8, key_rows.shape[1] // 8, 2)
        return block_terms(
            normed_vq, key_rows, value_rows, vid_grad, vid_lse, video_delta, word_rows, score_scale
        )

    starting = (
        jnp.zeros((head_count, local_video, head_dim), jnp.float32),
        jnp.zeros((head_count, audio_total, head_dim), jnp.float32),
        jnp.zeros((head_count, audio_total, head_dim), jnp.float32),
    )
    key_piece = lax.all_gather(normed_ak, "ctx", axis=1, tiled=True)
    value_piece = lax.all_gather(aud_value, "ctx", axis=1, tiled=True)
    piece_block = math.gcd(key_piece.shape[1], 512)

    def key_pass(block_index, totals):
        query_total, key_total, value_total = totals
        leading = block_index * piece_block
        key_rows = lax.dynamic_slice_in_dim(key_piece, leading, piece_block, 1)
        value_rows = lax.dynamic_slice_in_dim(value_piece, leading, piece_block, 1)
        dropped, score_grad = video_side(key_rows, value_rows, leading)
        query_total = query_total + score_scale * dot_plain(score_grad, key_rows)
        key_total = add_rows(key_total, score_scale * dot_cols(score_grad, normed_vq), leading)
        value_total = add_rows(value_total, dot_cols(dropped, vid_grad), leading)
        return (query_total, key_total, value_total)

    up_vq, key_partial, value_partial = lax.fori_loop(
        0, key_piece.shape[1] // piece_block, key_pass, starting
    )
    up_ak, audio_value_grad = (
        lax.psum_scatter(key_partial, "ctx", scatter_dimension=1, tiled=True),
        lax.psum_scatter(value_partial, "ctx", scatter_dimension=1, tiled=True),
    )
    starting_video = (
        jnp.zeros((head_count, local_video, head_dim), jnp.float32),
        jnp.zeros((head_count, local_video, head_dim), jnp.float32),
        jnp.zeros((head_count, audio_total, head_dim), jnp.float32),
    )
    query_piece = lax.all_gather(normed_aq, "ctx", axis=1, tiled=True)
    grad_piece = lax.all_gather(aud_grad, "ctx", axis=1, tiled=True)
    query_piece_block = math.gcd(query_piece.shape[1], 512)

    def query_pass(block_index, totals):
        key_total, value_total, query_total = totals
        leading = block_index * query_piece_block
        query_rows = lax.dynamic_slice_in_dim(query_piece, leading, query_piece_block, 1)
        grad_rows = lax.dynamic_slice_in_dim(grad_piece, leading, query_piece_block, 1)
        lse_rows = lax.dynamic_slice_in_dim(lse_whole, leading, query_piece_block, 1)
        delta_rows = lax.dynamic_slice_in_dim(delta_whole, leading, query_piece_block, 1)
        word_rows = lax.dynamic_slice_in_dim(aud_mask, leading, query_piece_block, 1)
        dropped, score_grad = block_terms(
            query_rows,
            normed_vk,
            vid_value,
            grad_rows,
            lse_rows,
            delta_rows,
            word_rows,
            score_scale,
        )
        value_total = value_total + dot_cols(dropped, grad_rows)
        key_total = key_total + score_scale * dot_cols(score_grad, query_rows)
        query_total = add_rows(query_total, score_scale * dot_plain(score_grad, normed_vk), leading)
        return (key_total, value_total, query_total)

    up_vk, video_value_grad, query_partial = lax.fori_loop(
        0, query_piece.shape[1] // query_piece_block, query_pass, starting_video
    )
    up_aq = lax.psum_scatter(query_partial, "ctx", scatter_dimension=1, tiled=True)
    weighted_vq, unit_vq, local_vq = norm_parts(vid_query, scale_vq, gain_vq, up_vq)
    weighted_ak, unit_ak, local_ak = norm_parts(aud_key, scale_ak, gain_ak, up_ak)
    weighted_aq, unit_aq, local_aq = norm_parts(aud_query, scale_aq, gain_aq, up_aq)
    weighted_vk, unit_vk, local_vk = norm_parts(vid_key, scale_vk, gain_vk, up_vk)
    product_vq, product_ak, product_aq, product_vk = lax.psum(
        (local_vq, local_ak, local_aq, local_vk), "head"
    )
    grad_vid_query = norm_finish(weighted_vq, unit_vq, scale_vq, product_vq, feature_count)
    grad_aud_key = norm_finish(weighted_ak, unit_ak, scale_ak, product_ak, feature_count)
    grad_aud_query = norm_finish(weighted_aq, unit_aq, scale_aq, product_aq, feature_count)
    grad_vid_key = norm_finish(weighted_vk, unit_vk, scale_vk, product_vk, feature_count)
    return (
        grad_vid_query,
        grad_vid_key,
        video_value_grad.astype(jnp.bfloat16),
        grad_aud_query,
        grad_aud_key,
        audio_value_grad.astype(jnp.bfloat16),
    )


def solution(mesh):
    return jax.shard_map(
        local,
        mesh=mesh,
        in_specs=(
            P("head", "ctx", None),
            P("head", "ctx", None),
            P("head", "ctx", None),
            P("head", "ctx", None),
            P("head", "ctx", None),
            P("head", "ctx"),
            P("head", "ctx", None),
            P("head", "ctx", None),
            P("head", "ctx", None),
            P("head", "ctx", None),
            P("head", "ctx", None),
            P("head", "ctx", None),
            P("head", "ctx"),
            P("head", None, "ctx"),
            P("head", None),
            P("head", None),
            P("head", None),
            P("head", None),
        ),
        out_specs=(
            P("head", "ctx", None),
            P("head", "ctx", None),
            P("head", "ctx", None),
            P("head", "ctx", None),
            P("head", "ctx", None),
            P("head", "ctx", None),
        ),
        check_vma=False,
    )
```

profile of v0, /device:TPU:1, one launch (start us, length us, event | category | flops | bytes accessed | tf_op | source)
XLA Modules:
  0.0 676.2 jit_solution(13393232645837971218)
XLA Ops:
  9.6 21.6 %all-reduce.1 = (f32[64]{0:T(128)S(1)}, f32[256]{0:T(256)S(1)}, f32[64]{0:T(128)S(1)}, f32[256]{0:T(256)S(1)}) all-reduce(f32[64]{0:T(128)S(1)} %get-tuple-element.648, f32[256]{0:T(256)S(1)} %get-tuple-element.646, f32[64]{0:T(128)S(1)} %get-tuple-element.649, f32[256]{0:T(256)S(1)} %get-tuple-element.647), channel_id=1, replica_groups=mesh['ctx'=32,'head'=8] {'head'}, use_global_device_ids=true, to_apply=%region_3.0 | all-reduce | flops 640 | bytes 5120 | tf_op jit(solution)/shard_map/psum | solution.py:100
  31.2 1.6 fusion.71
  33.6 1.6 fusion.77
  35.8 1.6 copy.45
  38.6 61.1 %all-gather.7.cloned.1.call-done = bf16[4,2048,128]{2,1,0:T(8,128)(2,1)} async-done(((bf16[4,64,128]{2,1,0:T(8,128)(2,1)}), bf16[4,2048,128]{2,1,0:T(8,128)(2,1)}) %all-gather.7.cloned.1.call-update) | async-done | bytes 2097168 | tf_op jit(solution)/shard_map/all_gather | solution.py:137
  99.7 66.4 %all-gather.9.cloned.1.call-done = bf16[4,2048,128]{2,1,0:T(8,128)(2,1)} async-done(((bf16[4,64,128]{2,1,0:T(8,128)(2,1)}), bf16[4,2048,128]{2,1,0:T(8,128)(2,1)}) %all-gather.9.cloned.1.call-update) | async-done | bytes 2097168 | tf_op jit(solution)/shard_map/all_gather | solution.py:138
  166.1 2.2 broadcast.158.clone
  168.3 2.2 broadcast.158.clone.1
  170.5 53.8 %while.38 = (s32[]{:T(128)}, f32[4,256,128]{2,1,0:T(8,128)}, f32[4,2048,128]{2,1,0:T(8,128)}, f32[4,2048,128]{2,1,0:T(8,128)}, bf16[4,2048,128]{2,1,0:T(8,128)(2...) while((s32[]{:T(128)}, f32[4,256,128]{2,1,0:T(8,128)}, ...), condition=%wide.region_6.0_spmd.clone, body=%wide.region_5.0_spmd.clone.sunk | while | flops 681705472 | bytes 28858916 | solution.py:152
  173.3 2.1 fusion.132
  175.4 2.8 fusion.134
  178.2 3.2 fusion.135
  181.4 2.5 fusion.133
  184.9 1.6 fusion.131
  186.6 2.1 fusion.132
  188.7 2.8 fusion.134
  191.5 3.2 fusion.135
  194.7 2.7 fusion.133
  200.1 2.1 fusion.132
  202.3 2.8 fusion.134
  205.0 3.2 fusion.135
  208.2 2.6 fusion.133
  212.0 1.5 fusion.131
  213.6 2.1 fusion.132
  215.8 2.8 fusion.134
  218.5 3.2 fusion.135
  221.7 2.6 fusion.133
  225.4 32.4 %all-gather.1 = f32[32,64,4]{1,2,0:T(4,128)S(1)} all-gather(f32[1,64,4]{1,2,0:T(4,128)S(1)} %bitcast.88), channel_id=1, replica_groups=mesh['ctx'=32,'head'=8] {'ctx'}, dimensions={0}, use_global_device_ids=true | all-gather | bytes 33792 | tf_op jit(solution)/shard_map/all_gather | solution.py:121
  257.9 30.9 %all-gather = f32[32,64,4]{1,2,0:T(4,128)S(1)} all-gather(f32[1,64,4]{1,2,0:T(4,128)S(1)} %bitcast.89), channel_id=1, replica_groups=mesh['ctx'=32,'head'=8] {'ctx'}, dimensions={0}, use_global_device_ids=true | all-gather | bytes 33792 | tf_op jit(solution)/shard_map/all_gather | solution.py:120
  288.9 10.3 %all-gather.13.cloned.1.call-done = bf16[4,2048,128]{2,1,0:T(8,128)(2,1)} async-done(((bf16[4,64,128]{2,1,0:T(8,128)(2,1)}), bf16[4,2048,128]{2,1,0:T(8,128)(2,1)}) %all-gather.13.cloned.1.call-update) | async-done | bytes 2097168 | tf_op jit(solution)/shard_map/all_gather | solution.py:165
  299.2 2.2 broadcast.158.clone.2
  301.4 73.1 %while.39 = (s32[]{:T(128)}, f32[4,256,128]{2,1,0:T(8,128)}, f32[4,256,128]{2,1,0:T(8,128)}, f32[4,2048,128]{2,1,0:T(8,128)}, bf16[4,2048,128]{2,1,0:T(8,128)(2,...) while((s32[]{:T(128)}, f32[4,256,128]{2,1,0:T(8,128)}, ...), condition=%wide.region_15.16_spmd.clone, body=%wide.region_14.15_spmd.clone.sunk | while | flops 681705472 | bytes 36238588 | solution.py:191
  303.9 1.6 broadcast_bitcast_fusion.2
  305.5 2.9 copy.52
  308.5 2.8 multiply_convert_fusion.6
  311.3 2.7 fusion.147
  314.0 2.5 fusion.146
  316.5 3.0 convolution_add_fusion.3
  321.9 1.6 broadcast_bitcast_fusion.2
  323.5 2.9 copy.52
  326.5 2.8 multiply_convert_fusion.6
  329.3 2.6 fusion.147
  332.0 2.7 fusion.146
  334.7 3.1 convolution_add_fusion.3
  340.3 1.6 broadcast_bitcast_fusion.2
  341.8 3.0 copy.52
  344.9 2.8 multiply_convert_fusion.6
  347.7 2.7 fusion.147
  350.3 2.7 fusion.146
  353.0 3.1 convolution_add_fusion.3
  358.6 1.6 broadcast_bitcast_fusion.2
  360.2 2.9 copy.52
  363.2 2.8 multiply_convert_fusion.6
  366.0 2.6 fusion.147
  368.7 2.7 fusion.146
  371.4 3.1 convolution_add_fusion.3
  375.3 1.8 convert_element_type.127
  377.6 42.7 %reduce-scatter.6.cloned.1.call-done = f32[4,64,128]{2,1,0:T(8,128)} async-done(((f32[4,2048,128]{2,1,0:T(8,128)}), f32[4,64,128]{2,1,0:T(8,128)}) %reduce-scatter.6.cloned.1.call-update) | async-done | bytes 131088 | tf_op jit(solution)/shard_map/reduce_scatter | solution.py:156
  421.4 122.2 %reduce-scatter.4.cloned.1.call-done = f32[4,64,128]{2,1,0:T(8,128)} async-done(((f32[4,2048,128]{2,1,0:T(8,128)}), f32[4,64,128]{2,1,0:T(8,128)}) %reduce-scatter.4.cloned.1.call-update) | async-done | bytes 131088 | tf_op jit(solution)/shard_map/reduce_scatter | solution.py:194
  544.7 20.2 %all-reduce = (f32[256]{0:T(256)S(1)}, f32[256]{0:T(256)S(1)}, f32[64]{0:T(128)S(1)}, f32[64]{0:T(128)S(1)}) all-reduce(f32[256]{0:T(256)S(1)} %fusion.54, f32[256]{0:T(256)S(1)} %fusion.60, f32[64]{0:T(128)S(1)} %fusion.78, f32[64]{0:T(128)S(1)} %fusion.72), channel_id=1, replica_groups=mesh['ctx'=32,'head'=8] {'head'}, use_global_device_ids=true, to_apply=%region_8.0 | all-reduce | flops 640 | bytes 5120 | tf_op jit(solution)/shard_map/psum | solution.py:199
  564.9 1.6 fusion.75
  566.6 1.6 fusion.81
  570.0 97.8 %reduce-scatter.8.cloned.1.call-done = f32[4,64,128]{2,1,0:T(8,128)} async-done(((f32[4,2048,128]{2,1,0:T(8,128)}), f32[4,64,128]{2,1,0:T(8,128)}) %reduce-scatter.8.cloned.1.call-update) | async-done | bytes 131088 | tf_op jit(solution)/shard_map/reduce_scatter | solution.py:157
  667.8 1.5 convert_element_type.130
  (152 shorter events, 29.4 us)
Async XLA Ops:
  7.2 30.2 %copy-start.8 = (bf16[4,256,128]{2,1,0:T(8,128)(2,1)S(1)}, bf16[4,256,128]{2,1,0:T(8,128)(2,1)}, u32[]{:S(2)}) copy-start(bf16[4,256,128]{2,1,0:T(8,128)(2,1)} %param.22) | copy-start | bytes 786436
  7.2 31.3 %copy-start.6 = (bf16[4,256,128]{2,1,0:T(8,128)(2,1)S(1)}, bf16[4,256,128]{2,1,0:T(8,128)(2,1)}, u32[]{:S(2)}) copy-start(bf16[4,256,128]{2,1,0:T(8,128)(2,1)} %param.23) | copy-start | bytes 786436
  7.2 30.2 %copy-start.20 = (f32[4,128]{1,0:T(4,128)S(1)}, f32[4,128]{1,0:T(4,128)}, u32[]{:S(2)}) copy-start(f32[4,128]{1,0:T(4,128)} %param.36) | copy-start | bytes 6148
  7.2 31.0 %copy-start.12 = (bf16[4,256,128]{2,1,0:T(8,128)(2,1)S(1)}, bf16[4,256,128]{2,1,0:T(8,128)(2,1)}, u32[]{:S(2)}) copy-start(bf16[4,256,128]{2,1,0:T(8,128)(2,1)} %param.25) | copy-start | bytes 786436
  7.2 31.0 %copy-start.13 = (bf16[4,256,128]{2,1,0:T(8,128)(2,1)S(1)}, bf16[4,256,128]{2,1,0:T(8,128)(2,1)}, u32[]{:S(2)}) copy-start(bf16[4,256,128]{2,1,0:T(8,128)(2,1)} %param.26) | copy-start | bytes 786436
  7.2 31.2 %copy-start.19 = (f32[4,128]{1,0:T(4,128)S(1)}, f32[4,128]{1,0:T(4,128)}, u32[]{:S(2)}) copy-start(f32[4,128]{1,0:T(4,128)} %param.39) | copy-start | bytes 6148
  7.2 92.5 %all-gather.7.cloned.1.call-start = ((), (), s32[]{:S(2)}) async-start(), calls=%async_computation.3 | async-start | bytes 2162688 | tf_op jit(solution)/shard_map/all_gather | solution.py:137
  32.7 133.3 %all-gather.9.cloned.1.call-start = ((), (), s32[]{:S(2)}) async-start(), calls=%async_computation.4 | async-start | bytes 2162688 | tf_op jit(solution)/shard_map/all_gather | solution.py:138
  33.5 255.4 %all-gather.11.cloned.1.call-start = ((), (), s32[]{:S(2)}) async-start(), calls=%async_computation.5 | async-start | bytes 2162688 | tf_op jit(solution)/shard_map/all_gather | solution.py:164
  35.1 264.1 %all-gather.13.cloned.1.call-start = ((), (), s32[]{:S(2)}) async-start(), calls=%async_computation.6 | async-start | bytes 2162688 | tf_op jit(solution)/shard_map/all_gather | solution.py:165
  35.7 384.6 %reduce-scatter.6.cloned.1.call-start = ((), (), s32[]{:S(2)}) async-start(), calls=%async_computation.8 | async-start | bytes 4325376 | tf_op jit(solution)/shard_map/reduce_scatter | solution.py:156
  168.3 2.2 copy-start.22
  170.5 1.1 copy-start.4
  175.4 2.8 copy-start.3
  181.4 2.5 copy-start.5
  181.4 2.5 copy-start.14
  183.8 1.1 copy-start.4
  188.7 2.8 copy-start.3
  194.7 2.7 copy-start.5
  194.7 2.7 copy-start.14
  197.4 1.1 copy-start.4
  202.2 2.8 copy-start.3
  208.2 2.6 copy-start.5
  208.2 2.6 copy-start.14
  210.9 1.1 copy-start.4
  215.8 2.8 copy-start.3
  221.7 2.6 copy-start.5
  221.7 2.6 copy-start.14
  224.4 0.8 copy-start.15
  224.4 0.9 copy-start.16
  224.4 33.5 %copy-start.21 = (f32[4,64]{1,0:T(4,128)S(1)}, f32[4,64]{1,0:T(4,128)}, u32[]{:S(2)}) copy-start(f32[4,64]{1,0:T(4,128)} %param.34) | copy-start | bytes 3076
  224.4 319.2 %reduce-scatter.4.cloned.1.call-start = ((), (), s32[]{:S(2)}) async-start(), calls=%async_computation.7 | async-start | bytes 4325376 | tf_op jit(solution)/shard_map/reduce_scatter | solution.py:194
  314.0 2.5 copy-start
  332.0 2.7 copy-start
  350.3 2.7 copy-start
  368.7 2.7 copy-start
  374.5 293.3 %reduce-scatter.8.cloned.1.call-start = ((), (), s32[]{:S(2)}) async-start(), calls=%async_computation.9 | async-start | bytes 4325376 | tf_op jit(solution)/shard_map/reduce_scatter | solution.py:157
  374.6 2.6 copy-start.2
  374.6 2.6 copy-start.9
  374.6 2.8 copy-start.1
  374.6 2.8 copy-start.7
  375.3 45.0 %copy-start.10 = (bf16[4,64,128]{2,1,0:T(8,128)(2,1)S(1)}, bf16[4,64,128]{2,1,0:T(8,128)(2,1)}, u32[]{:S(2)}) copy-start(bf16[4,64,128]{2,1,0:T(8,128)(2,1)} %param.30) | copy-start | bytes 196612
  375.3 45.0 %copy-start.17 = (f32[4,128]{1,0:T(4,128)S(1)}, f32[4,128]{1,0:T(4,128)}, u32[]{:S(2)}) copy-start(f32[4,128]{1,0:T(4,128)} %param.37) | copy-start | bytes 6148
  375.3 168.3 %copy-start.11 = (bf16[4,64,128]{2,1,0:T(8,128)(2,1)S(1)}, bf16[4,64,128]{2,1,0:T(8,128)(2,1)}, u32[]{:S(2)}) copy-start(bf16[4,64,128]{2,1,0:T(8,128)(2,1)} %param.29) | copy-start | bytes 196612
  375.3 168.3 %copy-start.18 = (f32[4,128]{1,0:T(4,128)S(1)}, f32[4,128]{1,0:T(4,128)}, u32[]{:S(2)}) copy-start(f32[4,128]{1,0:T(4,128)} %param.38) | copy-start | bytes 6148
Sparse Core Ops, SparseCore 0:
  32.9 66.7 all-gather.6
  101.6 64.4 all-gather.8
  168.5 64.4 all-gather.10
  234.7 64.3 all-gather.12
  301.6 118.6 reduce-scatter.5
  422.7 120.8 reduce-scatter.3
  546.1 121.6 reduce-scatter.7
where the time goes:
time: 681 us; the launch traced here: 676 us
  waiting for transfers between devices  402 us (59%)
  blocking collectives  105 us (15%)
  matrix products  99.4 us (15%)
  local copies, waits for them, and re-layouts  36.5 us (5%)
  other arithmetic  17.8 us (3%)
  between operations  14.4 us (2%)
    reduce_scatter x1, waiting for transfers between devices, local(): lax.psum_scatter(query_partial, 'ctx', scatter_dimension=1, tiled=True)  122 us
    reduce_scatter x1, waiting for transfers between devices, local(): lax.psum_scatter(value_partial, 'ctx', scatter_dimension=1, tiled=True)  97.8 us
    all_gather x1, waiting for transfers between devices, local(): value_piece = lax.all_gather(aud_value, 'ctx', axis=1, tiled=True)  66.4 us
    all_gather x1, waiting for transfers between devices, local(): key_piece = lax.all_gather(normed_ak, 'ctx', axis=1, tiled=True)  61.1 us
    dot_general x16, matrix products, dot_cols(): lax.dot_general(left, right, (((1,), (1,)), ((0,), (0,))), preferred_elem...  46.8 us
    reduce_scatter x1, waiting for transfers between devices, local(): lax.psum_scatter(key_partial, 'ctx', scatter_dimension=1, tiled=True)  42.7 us
    all_gather x1, blocking collectives, local(): lax.all_gather(audio_delta, 'ctx', axis=1, tiled=True)  32.4 us
    dot_general x16, matrix products, dot_rows(): lax.dot_general(left, right, (((2,), (2,)), ((0,), (0,))), preferred_elem...  31.6 us
  transfers between devices with their start and end apart: 7, of which 6 were waited for; matrix products, arithmetic and copies ran while one was open for 22% of the time, Pallas kernels for 0%

commit v1 on v0

v1 whole, which is shorter than its diff:
```python
import functools
import math

import jax
import jax.numpy as jnp
from jax import lax
from jax.experimental import pallas as pl
from jax.experimental.pallas import tpu as pltpu
from jax.sharding import Mesh
from jax.sharding import PartitionSpec as P

EPS = 1e-06
LOG2E = math.log2(math.e)
F32 = jnp.float32
BF16 = jnp.bfloat16
PLANES, NEAR, CORES, HEAD_GROUPS = 8, 2, 2, 8
QUAD = NEAR * CORES
QUAD_AXES = ("near", "core")
CTX_AXES = ("plane", "near", "core")


def dot_nt(left, right):
    return lax.dot_general(left, right, (((1,), (1,)), ((), ())), preferred_element_type=F32)


def dot_nn(left, right):
    return lax.dot_general(left, right, (((1,), (0,)), ((), ())), preferred_element_type=F32)


def dot_tn(left, right):
    return lax.dot_general(left, right, (((0,), (0,)), ((), ())), preferred_element_type=F32)


def keep_rows(words):
    wide = words.astype(jnp.int32)
    return jnp.concatenate([jnp.bitwise_and(wide, 1 << bit) != 0 for bit in range(8)], axis=0)


def probs_and_scores(keys, values, queries, twice_grad, lse2, delta, kept, coefficient):
    probs = jnp.exp2(dot_nt(keys, queries) * coefficient - lse2)
    dropped = jnp.where(kept, probs, 0.0).astype(BF16)
    prob_grad = jnp.where(kept, dot_nt(values, twice_grad), 0.0)
    return dropped, (probs * (prob_grad - delta)).astype(BF16)


def attention_kernel(
    aud_k, aud_v, aud_q, aud_g, aud_l, aud_d, vid_k, vid_v, vid_q, vid_g, vid_l, vid_d,
    vid_words, aud_words, aud_out, vid_out, sum_k, sum_v, sum_q, *, scale
):
    step = pl.program_id(0)
    coefficient = scale * LOG2E

    @pl.when(step == 0)
    def _():
        sum_k[...] = jnp.zeros_like(sum_k)
        sum_v[...] = jnp.zeros_like(sum_v)
        sum_q[...] = jnp.zeros_like(sum_q)

    keys, values, queries, grads = aud_k[0], aud_v[0], aud_q[0], aud_g[0]
    kept = keep_rows(jnp.concatenate([vid_words[i] for i in range(vid_words.shape[0])], axis=1))
    dropped, score_grad = probs_and_scores(
        keys, values, vid_q[...], vid_g[...], vid_l[...], vid_d[...], kept, coefficient
    )
    aud_out[0, 0] = (dot_nn(score_grad, vid_q[...]) * scale).astype(aud_out.dtype)
    aud_out[0, 1] = dot_nn(dropped, vid_g[...]).astype(aud_out.dtype)
    sum_q[...] += dot_tn(score_grad, keys)
    kept = keep_rows(aud_words[...].reshape(-1, aud_words.shape[2]))
    dropped, score_grad = probs_and_scores(
        vid_k[...], vid_v[...], queries, grads, aud_l[0], aud_d[0], kept, coefficient
    )
    sum_v[...] += dot_nn(dropped, grads)
    sum_k[...] += dot_nn(score_grad, queries)
    aud_out[0, 2] = (dot_tn(score_grad, vid_k[...]) * scale).astype(aud_out.dtype)

    @pl.when(step == pl.num_programs(0) - 1)
    def _():
        vid_out[0] = (sum_k[...] * scale).astype(vid_out.dtype)
        vid_out[1] = sum_v[...].astype(vid_out.dtype)
        vid_out[2] = (sum_q[...] * scale).astype(vid_out.dtype)


def attention(aud, aud_rows, vid, vid_rows, vid_words, aud_words, scale):
    planes, rows, dim = aud[0].shape
    vid_count = vid[0].shape[0]
    whole = pl.BlockSpec((vid_count, dim), lambda c: (0, 0))
    line = pl.BlockSpec((1, vid_count), lambda c: (0, 0))
    block = pl.BlockSpec((1, rows, dim), lambda c: (c, 0, 0))
    block_line = pl.BlockSpec((1, 1, rows), lambda c: (c, 0, 0))
    pairs = 2 * planes * rows * vid_count
    return pl.pallas_call(
        functools.partial(attention_kernel, scale=scale),
        grid=(planes,),
        in_specs=[block] * 4 + [block_line] * 2 + [whole] * 4 + [line] * 2 + [
            pl.BlockSpec((vid_words.shape[0], rows // 8, vid_words.shape[2]), lambda c: (0, c, 0)),
            pl.BlockSpec((aud_words.shape[0], aud_words.shape[1], rows), lambda c: (0, 0, c)),
        ],
        out_specs=[
            pl.BlockSpec((1, 3, rows, dim), lambda c: (c, 0, 0, 0)),
            pl.BlockSpec((3, vid_count, dim), lambda c: (0, 0, 0)),
        ],
        out_shape=[
            jax.ShapeDtypeStruct((planes, 3, rows, dim), BF16),
            jax.ShapeDtypeStruct((3, vid_count, dim), BF16),
        ],
        scratch_shapes=[pltpu.VMEM((vid_count, dim), F32)] * 3,
        compiler_params=pltpu.CompilerParams(vmem_limit_bytes=56 * 2**20),
        cost_estimate=pl.CostEstimate(
            flops=10 * pairs * dim, bytes_accessed=8 * 2**20, transcendentals=pairs
        ),
    )(*aud, *aud_rows, *vid, *vid_rows, vid_words, aud_words)


def over_heads(sums):
    return jnp.sum(
        lax.all_to_all(
            jnp.broadcast_to(sums[None], (HEAD_GROUPS,) + sums.shape), "head", 0, 0, tiled=True
        ),
        axis=0,
    )


def square_sums(tokens):
    values = tokens.astype(F32)
    return jnp.sum(values * values, axis=(0, 2))


def bits_first(rows):
    split = rows.reshape(rows.shape[:-2] + (rows.shape[-2] // 8, 8, rows.shape[-1]))
    return jnp.swapaxes(split, -3, -2)


def to_quad(rows):
    return lax.all_to_all(rows, QUAD_AXES, 0, 0, tiled=True)


def normalize(tokens, scales, gain_row):
    return (tokens.astype(F32) * scales[..., None] * gain_row).astype(BF16)


def norm_parts(tokens, scales, gain_rows, upstream):
    weighted = upstream.astype(F32) * gain_rows[:, None, :]
    unit_rows = tokens.astype(F32) * scales[None, :, None]
    return weighted, unit_rows, jnp.sum(weighted * unit_rows, axis=(0, 2))


def norm_finish(weighted, unit_rows, scales, mean_term):
    return (scales[None, :, None] * (weighted - unit_rows * mean_term[None, :, None])).astype(BF16)


def local(
    vid_query, vid_key, vid_value, vid_out, vid_grad, vid_lse, vid_mask,
    aud_query, aud_key, aud_value, aud_out, aud_grad, aud_lse, aud_mask,
    gain_vq, gain_ak, gain_aq, gain_vk,
):
    heads, vid_rows, dim = vid_query.shape
    aud_rows = aud_query.shape[1]
    vid_words, aud_words = vid_rows // 8, aud_rows // 8
    plane_rows, quad_rows = QUAD * aud_rows, QUAD * vid_rows
    feature_count = HEAD_GROUPS * heads * dim
    scale = dim**-0.5

    audio = jnp.stack(
        [
            bits_first(aud_key).reshape(aud_key.shape),
            bits_first(aud_value).reshape(aud_value.shape),
            aud_query,
            aud_grad + aud_grad,
        ],
        axis=1,
    )
    audio = jnp.swapaxes(to_quad(audio), 0, 1)
    by_word = audio[:2].reshape(2, QUAD, 8, aud_words, dim).swapaxes(1, 2)
    audio = jnp.concatenate(
        [by_word.reshape(2, plane_rows, dim), audio[2:].reshape(2, plane_rows, dim)]
    )
    audio = lax.all_gather(audio, "plane", axis=0, tiled=False)

    sums = jnp.concatenate(
        [square_sums(vid_query), square_sums(vid_key), square_sums(aud_key), square_sums(aud_query)]
    )
    scales = lax.rsqrt(over_heads(sums) / feature_count + EPS)
    cuts = (vid_rows, 2 * vid_rows, 2 * vid_rows + aud_rows)
    scale_vq, scale_vk, scale_ak, scale_aq = jnp.split(scales, cuts)

    video = jnp.stack(
        [bits_first(vid_key).reshape(vid_key.shape), bits_first(vid_value).reshape(vid_key.shape),
         vid_query, vid_grad + vid_grad], axis=1,
    )
    video = jnp.swapaxes(to_quad(video), 0, 1)
    by_word = video[:2].reshape(2, QUAD, 8, vid_words, dim).swapaxes(1, 2)
    vid_k, vid_v = by_word.reshape(2, quad_rows, dim)
    vid_q, vid_g = video[2:].reshape(2, quad_rows, dim)
    words_v = to_quad(jnp.swapaxes(vid_mask.astype(jnp.int16), 1, 2))
    words_a = to_quad(jnp.swapaxes(aud_mask.astype(jnp.int16), 1, 2))

    delta_v = jnp.sum(vid_grad.astype(F32) * vid_out.astype(F32), axis=2)
    delta_a = jnp.sum(aud_grad.astype(F32) * aud_out.astype(F32), axis=2)

    def per_head(lse, delta, scale_a, scale_b):
        return jnp.stack(
            [lse * LOG2E, delta, jnp.broadcast_to(scale_a, lse.shape), jnp.broadcast_to(scale_b, lse.shape)],
            axis=1,
        )

    small_a = per_head(aud_lse, delta_a, scale_ak, scale_aq)
    small_a = lax.all_to_all(
        jnp.broadcast_to(small_a[None], (PLANES,) + small_a.shape).reshape(PLANES * QUAD, 4, aud_rows),
        CTX_AXES, 0, 0, tiled=True,
    )
    small_a = small_a.reshape(PLANES, QUAD, 4, aud_rows).swapaxes(1, 2)
    lse_a, sums_a, whole_ak, whole_aq = jnp.moveaxis(small_a, 1, 0)
    whole_ak = whole_ak.reshape(PLANES, QUAD, aud_words, 8).transpose(0, 3, 1, 2).reshape(PLANES, plane_rows)
    whole_aq = whole_aq.reshape(PLANES, plane_rows)
    small_v = jnp.swapaxes(to_quad(per_head(vid_lse, delta_v, scale_vk, scale_vq)), 0, 1)
    lse_v, sums_v, whole_vk, whole_vq = small_v
    whole_vk = whole_vk.reshape(QUAD, vid_words, 8).transpose(2, 0, 1).reshape(quad_rows)
    whole_vq = whole_vq.reshape(quad_rows)

    own = lax.axis_index(QUAD_AXES)

    def own_gain(gain):
        return lax.dynamic_index_in_dim(gain, own, 0, keepdims=False)

    aud_sets = (
        normalize(audio[:, 0], whole_ak, own_gain(gain_ak)),
        audio[:, 1],
        normalize(audio[:, 2], whole_aq, own_gain(gain_aq)),
        audio[:, 3],
    )
    vid_sets = (
        normalize(vid_k, whole_vk, own_gain(gain_vk)),
        vid_v,
        normalize(vid_q, whole_vq, own_gain(gain_vq)),
        vid_g,
    )
    aud_parts, vid_parts = attention(
        aud_sets,
        (lse_a.reshape(PLANES, 1, plane_rows), sums_a.reshape(PLANES, 1, plane_rows)),
        vid_sets,
        (lse_v.reshape(1, quad_rows), sums_v.reshape(1, quad_rows)),
        words_v, words_a, scale,
    )
    aud_total = lax.psum_scatter(aud_parts, "plane", scatter_dimension=0, tiled=True)[0]

    def back(parts, words):
        by_bit = parts[:2].reshape(2, 8, QUAD, words, dim).transpose(2, 0, 3, 1, 4)
        by_row = parts[2].reshape(QUAD, 1, 8 * words, dim)
        home = jnp.concatenate([by_bit.reshape(QUAD, 2, 8 * words, dim), by_row], axis=1)
        return jnp.swapaxes(to_quad(home), 0, 1)

    up_vk, grad_vv, up_vq = back(vid_parts, vid_words)
    weighted_vq, unit_vq, local_vq = norm_parts(vid_query, scale_vq, gain_vq, up_vq)
    weighted_vk, unit_vk, local_vk = norm_parts(vid_key, scale_vk, gain_vk, up_vk)
    mean_vq, mean_vk = over_heads(jnp.stack([local_vq, local_vk])) / feature_count
    grad_vid_query = norm_finish(weighted_vq, unit_vq, scale_vq, mean_vq)
    grad_vid_key = norm_finish(weighted_vk, unit_vk, scale_vk, mean_vk)

    up_ak, grad_av, up_aq = back(aud_total, aud_words)
    weighted_ak, unit_ak, local_ak = norm_parts(aud_key, scale_ak, gain_ak, up_ak)
    weighted_aq, unit_aq, local_aq = norm_parts(aud_query, scale_aq, gain_aq, up_aq)
    mean_ak, mean_aq = over_heads(jnp.stack([local_ak, local_aq])) / feature_count
    grad_aud_key = norm_finish(weighted_ak, unit_ak, scale_ak, mean_ak)
    grad_aud_query = norm_finish(weighted_aq, unit_aq, scale_aq, mean_aq)
    return grad_vid_query, grad_vid_key, grad_vv, grad_aud_query, grad_aud_key, grad_av


def solution(mesh):
    fine = Mesh(
        mesh.devices.reshape(PLANES, NEAR, CORES, HEAD_GROUPS), ("plane", "near", "core", "head")
    )
    rows, lines, gain = P("head", CTX_AXES, None), P("head", CTX_AXES), P("head", None)
    return jax.shard_map(
        local,
        mesh=fine,
        in_specs=(rows,) * 5 + (lines, rows) + (rows,) * 5 + (lines, P("head", None, CTX_AXES)) + (gain,) * 4,
        out_specs=(rows,) * 6,
        check_vma=False,
    )
```

time: 681 us -> 190 us (0.28)
  waiting for transfers between devices: 402 us -> 49.6 us
  matrix products: 99.4 us -> 0 us
  blocking collectives: 105 us -> 14.3 us
  starting transfers between devices: 0.28 us -> 56.6 us
  local copies, waits for them, and re-layouts: 36.5 us -> 18.1 us
  Pallas kernels: 0 us -> 17.1 us
    reduce_scatter x3 -> x1, waiting for transfers between devices: 263 us -> 2.44 us  [local(): lax.psum_scatter(aud_parts, 'plane', scatter_dimension=0, tiled=True)[0]]
    all_gather x4 -> x1, waiting for transfers between devices: 138 us -> 0.01 us  [local(): audio = lax.all_gather(audio, 'plane', axis=0, tiled=False)]
    dot_general x40 -> x0, matrix products: 99.4 us -> none  [the longest x16 46.8 us: dot_cols(): lax.dot_general(left, right, (((1,), (1,)), ((0,), (0,))), preferred_elem...]
    all_gather x2 -> x0, blocking collectives: 63.3 us -> none  [the longest x1 32.4 us: local(): lax.all_gather(audio_delta, 'ctx', axis=1, tiled=True)]
    all_to_all x0 -> x10, starting transfers between devices: none -> 56.6 us  [the longest x6 32.6 us: to_quad(): return lax.all_to_all(rows, QUAD_AXES, 0, 0, tiled=True)]
    all_to_all x0 -> x10, waiting for transfers between devices: none -> 47.1 us  [the longest x6 23.4 us: to_quad(): return lax.all_to_all(rows, QUAD_AXES, 0, 0, tiled=True)]
    psum x2 -> x0, blocking collectives: 41.8 us -> none  [the longest x1 21.6 us: local(): lax.psum((square_sums(vid_query), square_sums(aud_key), square_sums(aud_q...]
    shift_right_arithmetic x24 -> x0, local copies, waits for them, and re-layouts: 18.8 us -> none  [unpack_bits(): jnp.right_shift(word_rows[..., None], shifts)]
  transfers between devices with their start and end apart: 7 -> 12, of which waited for: 6 -> 11; matrix products, arithmetic and copies ran while one was open for 22% -> 14% of each run, Pallas kernels for 0% -> 0%
where the time goes in v1:
time: 190 us; the launch traced here: 188 us
  starting transfers between devices  56.6 us (30%)
  waiting for transfers between devices  49.6 us (26%)
  other arithmetic  18.2 us (10%)
  local copies, waits for them, and re-layouts  18.1 us (10%)
  Pallas kernels  17.1 us (9%)
  between operations  14.5 us (8%)
  blocking collectives  14.3 us (8%)
    all_to_all x6, starting transfers between devices, to_quad(): return lax.all_to_all(rows, QUAD_AXES, 0, 0, tiled=True)  32.6 us
    all_to_all x6, waiting for transfers between devices, to_quad(): return lax.all_to_all(rows, QUAD_AXES, 0, 0, tiled=True)  23.4 us
    pallas_call x1, Pallas kernels, attention(): pl.pallas_call(functools.partial(attention_kernel, scale=scale), grid=(pl...  17.1 us
    all_to_all x3, waiting for transfers between devices, over_heads(): lax.all_to_all(jnp.broadcast_to(sums[None], (HEAD_GROUPS,) + sums.shape),...  15.6 us
    all_to_all x3, starting transfers between devices, over_heads(): lax.all_to_all(jnp.broadcast_to(sums[None], (HEAD_GROUPS,) + sums.shape),...  14.6 us
    all_to_all x1, blocking collectives, to_quad(): return lax.all_to_all(rows, QUAD_AXES, 0, 0, tiled=True)  14.3 us
    all_to_all x1, starting transfers between devices, local(): lax.all_to_all(jnp.broadcast_to(small_a[None], (PLANES,) + small_a.shape)...  9.35 us
    all_to_all x1, waiting for transfers between devices, local(): lax.all_to_all(jnp.broadcast_to(small_a[None], (PLANES,) + small_a.shape)...  8.1 us
  transfers between devices with their start and end apart: 12, of which 11 were waited for; matrix products, arithmetic and copies ran while one was open for 14% of the time, Pallas kernels for 0%

profile of v1, /device:TPU:1, one launch (start us, length us, event | category | flops | bytes accessed | tf_op | source)
XLA Modules:
  0.0 188.4 jit_solution(414857939063029563)
XLA Ops:
  7.2 0.9 copy.150
  8.1 0.9 copy.151
  9.0 0.8 add_bitcast_fusion.1
  9.8 1.6 pad_maximum_fusion.2
  11.4 6.6 %all-to-all-start.1 = ((bf16[4,4,64,128]{3,2,1,0:T(8,128)(2,1)}), bf16[4,4,64,128]{3,2,1,0:T(8,128)(2,1)S(1)}, u32[]{:S(2)}, u32[]{:S(2)}) async-start(bf16[4,4,64,128]{3,2,1,0:T(8,128)(2,1)} %pad_maximum_fusion.2), calls=%async_computation.1 | async-start | bytes 524288 | tf_op jit(solution)/shard_map/all_to_all | solution.py:133
  18.0 1.0 fusion.34
  19.1 1.1 fusion.16
  20.1 1.1 fusion.17
  21.5 1.1 pad_maximum_fusion
  22.6 0.6 all-to-all-done.1
  23.2 0.6 broadcast_in_dim.8
  23.8 4.9 %all-to-all-start = ((f32[8,1,640]{2,1,0:T(1,128)}), f32[8,1,640]{2,1,0:T(1,128)S(1)}, u32[]{:S(2)}, u32[]{:S(2)}) async-start(f32[8,1,640]{2,1,0:T(1,128)} %broadcast_in_dim.8), calls=%async_computation | async-start | bytes 40960 | tf_op jit(solution)/shard_map/all_to_all | solution.py:115
  28.9 0.7 pad_maximum_fusion.3
  29.7 0.2 multiply_reduce_fusion
  29.9 0.9 convert_bitcast_fusion
  31.0 0.3 copy.124
  31.3 4.0 %all-to-all-done = f32[8,1,640]{2,1,0:T(1,128)S(1)} async-done(((f32[8,1,640]{2,1,0:T(1,128)}), f32[8,1,640]{2,1,0:T(1,128)S(1)}, u32[]{:S(2)}, u32[]{:S(2)}) %all-to-all-start) | async-done | bytes 20512 | tf_op jit(solution)/shard_map/all_to_all | solution.py:115
  35.4 0.6 pad_maximum_fusion.5
  36.0 5.5 %all-to-all-start.4 = ((f32[4,4,256]{2,1,0:T(4,128)}), f32[4,4,256]{2,1,0:T(4,128)S(1)}, u32[]{:S(2)}, u32[]{:S(2)}) async-start(f32[4,4,256]{2,1,0:T(4,128)} %pad_maximum_fusion.5), calls=%async_computation.4 | async-start | bytes 32768 | tf_op jit(solution)/shard_map/all_to_all | solution.py:133
  41.7 0.7 reshape.137
  42.4 2.3 %all-to-all-done.4 = f32[4,4,256]{2,1,0:T(4,128)S(1)} async-done(((f32[4,4,256]{2,1,0:T(4,128)}), f32[4,4,256]{2,1,0:T(4,128)S(1)}, u32[]{:S(2)}, u32[]{:S(2)}) %all-to-all-start.4) | async-done | bytes 16416 | tf_op jit(solution)/shard_map/all_to_all | solution.py:133
  44.7 9.4 %all-to-all-start.2 = ((f32[32,1,256]{2,1,0:T(1,128)}), f32[32,1,256]{2,1,0:T(1,128)S(1)}, u32[]{:S(2)}, u32[]{:S(2)}) async-start(f32[32,1,256]{2,1,0:T(1,128)} %reshape.137), calls=%async_computation.2 | async-start | bytes 65536 | tf_op jit(solution)/shard_map/all_to_all | solution.py:206
  54.1 8.1 %all-to-all-done.2 = f32[32,1,256]{2,1,0:T(1,128)S(1)} async-done(((f32[32,1,256]{2,1,0:T(1,128)}), f32[32,1,256]{2,1,0:T(1,128)S(1)}, u32[]{:S(2)}, u32[]{:S(2)}) %all-to-all-start.2) | async-done | bytes 32800 | tf_op jit(solution)/shard_map/all_to_all | solution.py:206
  62.2 3.9 %all-to-all-start.3 = ((bf16[4,4,256,128]{3,2,1,0:T(8,128)(2,1)}), bf16[4,4,256,128]{3,2,1,0:T(8,128)(2,1)S(1)}, u32[]{:S(2)}, u32[]{:S(2)}) async-start(bf16[4,4,256,128]{3,2,1,0:T(8,128)(2,1)} %pad_maximum_fusion), calls=%async_computation.3 | async-start | bytes 2097152 | tf_op jit(solution)/shard_map/all_to_all | solution.py:133
  66.1 0.9 convert_bitcast_fusion.1
  66.9 0.6 fusion.43
  67.8 0.5 broadcast.18
  68.4 0.7 reduce.3
  69.2 0.7 reshape_unstack.20.aud_d
  69.9 0.7 reshape_unstack.19.aud_l
  71.0 8.6 %all-to-all-done.3 = bf16[4,4,256,128]{3,2,1,0:T(8,128)(2,1)S(1)} async-done(((bf16[4,4,256,128]{3,2,1,0:T(8,128)(2,1)}), bf16[4,4,256,128]{3,2,1,0:T(8,128)(2,1)S(1)}, u32[]{:S(2)}, u32[]{:S(2)}) %all-to-all-start.3) | async-done | bytes 1048608 | tf_op jit(solution)/shard_map/all_to_all | solution.py:133
  79.7 4.3 %all-to-all-start.6 = ((s16[4,32,2048]{2,1,0:T(8,128)(2,1)}), s16[4,32,2048]{2,1,0:T(8,128)(2,1)S(1)}, u32[]{:S(2)}, u32[]{:S(2)}) async-start(s16[4,32,2048]{2,1,0:T(8,128)(2,1)} %convert_bitcast_fusion), calls=%async_computation.6 | async-start | bytes 1048576 | tf_op jit(solution)/shard_map/all_to_all | solution.py:133
  84.1 0.7 fusion.40
  84.8 0.7 fusion.41
  85.6 0.9 fusion.21.vid_k
  86.5 0.9 fusion.19.vid_q
  87.4 4.6 %all-to-all-done.6.aud_words = s16[4,32,2048]{2,1,0:T(8,128)(2,1)S(1)} async-done(((s16[4,32,2048]{2,1,0:T(8,128)(2,1)}), s16[4,32,2048]{2,1,0:T(8,128)(2,1)S(1)}, u32[]{:S(2)}, u32[]{:S(2)}) %all-to-all-start.6) | async-done | bytes 524320 | tf_op jit(solution)/shard_map/all_to_all | solution.py:133
  92.0 4.3 %all-to-all-start.5 = ((s16[4,256,256]{2,1,0:T(8,128)(2,1)}), s16[4,256,256]{2,1,0:T(8,128)(2,1)S(1)}, u32[]{:S(2)}, u32[]{:S(2)}) async-start(s16[4,256,256]{2,1,0:T(8,128)(2,1)} %convert_bitcast_fusion.1), calls=%async_computation.5 | async-start | bytes 1048576 | tf_op jit(solution)/shard_map/all_to_all | solution.py:133
  96.3 2.4 %slice_bitcast_fusion = (bf16[8,256,128]{2,1,0:T(8,128)(2,1)}, bf16[8,256,128]{2,1,0:T(8,128)(2,1)}) fusion(bf16[8,4,256,128]{3,2,1,0:T(8,128)(2,1)} %bitcast.167), kind=kLoop, calls=%fused_computation.26 | loop fusion | bytes 2097152 | tf_op jit(solution)/shard_map/squeeze | solution.py:228
  98.7 1.5 fusion.1
  100.3 4.0 %all-to-all-done.5.vid_words = s16[4,256,256]{2,1,0:T(8,128)(2,1)S(1)} async-done(((s16[4,256,256]{2,1,0:T(8,128)(2,1)}), s16[4,256,256]{2,1,0:T(8,128)(2,1)S(1)}, u32[]{:S(2)}, u32[]{:S(2)}) %all-to-all-start.5) | async-done | bytes 524320 | tf_op jit(solution)/shard_map/all_to_all | solution.py:133
  104.2 0.8 copy-done.10
  105.1 17.1 %shard_map.217 = (bf16[8,3,256,128]{3,2,1,0:T(8,128)(2,1)}, bf16[3,1024,128]{2,1,0:T(8,128)(2,1)}) custom-call(bf16[8,256,128]{2,1,0:T(8,128)(2,1)} %get-tuple-element.17.aud_k, bf16[8,256,128]{2,1,0:T(8,128)(2,1)} %get-tuple-element.15.aud_v, bf16[8,256,128]{2,1,0:T(8,128)(2,1)} %get-tuple-element.16.aud_q, bf16[8,256,128]{2,1,0:T(8,128)(2,1)} %get-tuple-element.14.aud_g, ...), custom_call_target="tpu_custom_call" | custom-call | flops 5368709120 | bytes 8388608 | tf_op jit(solution)/shard_map/pallas_call | solution.py:90
  122.2 1.0 slice.50
  123.4 0.3 copy.145
  123.8 14.3 %all_to_all.56 = bf16[4,3,256,128]{3,2,1,0:T(8,128)(2,1)S(1)} all-to-all(bf16[4,3,256,128]{3,2,1,0:T(8,128)(2,1)S(1)} %pad_maximum_fusion.1), channel_id=1, replica_groups=mesh['plane'=8,'near'=2,'core'=2,'head'=8] {'near','core'}, dimensions={0} | all-to-all | bytes 1572864 | tf_op jit(solution)/shard_map/all_to_all | solution.py:133
  138.1 0.3 fusion.12
  138.4 0.6 broadcast_in_dim.10
  139.1 3.3 %all-to-all-start.8 = ((f32[8,2,256]{2,1,0:T(2,128)}), f32[8,2,256]{2,1,0:T(2,128)S(1)}, u32[]{:S(2)}, u32[]{:S(2)}) async-start(f32[8,2,256]{2,1,0:T(2,128)} %broadcast_in_dim.10), calls=%async_computation.8 | async-start | bytes 32768 | tf_op jit(solution)/shard_map/all_to_all | solution.py:115
  142.4 0.7 slice_bitcast_fusion.4
  143.1 5.8 %all-to-all-done.8 = f32[8,2,256]{2,1,0:T(2,128)S(1)} async-done(((f32[8,2,256]{2,1,0:T(2,128)}), f32[8,2,256]{2,1,0:T(2,128)S(1)}, u32[]{:S(2)}, u32[]{:S(2)}) %all-to-all-start.8) | async-done | bytes 16416 | tf_op jit(solution)/shard_map/all_to_all | solution.py:115
  148.9 2.4 %reduce-scatter.2.cloned.1.call-done = bf16[1,3,256,128]{3,2,1,0:T(8,128)(2,1)} async-done(((bf16[8,3,256,128]{3,2,1,0:T(8,128)(2,1)}), bf16[1,3,256,128]{3,2,1,0:T(8,128)(2,1)}) %reduce-scatter.2.cloned.1.call-update) | async-done | bytes 196624 | tf_op jit(solution)/shard_map/reduce_scatter | solution.py:243
  151.4 0.9 slice.60
  152.4 0.8 slice.61
  153.2 0.7 pad_maximum_fusion.4
  153.9 8.0 %all-to-all-start.9 = ((bf16[4,3,64,128]{3,2,1,0:T(8,128)(2,1)}), bf16[4,3,64,128]{3,2,1,0:T(8,128)(2,1)S(1)}, u32[]{:S(2)}, u32[]{:S(2)}) async-start(bf16[4,3,64,128]{3,2,1,0:T(8,128)(2,1)} %pad_maximum_fusion.4), calls=%async_computation.10 | async-start | bytes 393216 | tf_op jit(solution)/shard_map/all_to_all | solution.py:133
  161.9 1.1 fusion.11
  163.0 3.4 %all-to-all-done.9 = bf16[4,3,64,128]{3,2,1,0:T(8,128)(2,1)S(1)} async-done(((bf16[4,3,64,128]{3,2,1,0:T(8,128)(2,1)}), bf16[4,3,64,128]{3,2,1,0:T(8,128)(2,1)S(1)}, u32[]{:S(2)}, u32[]{:S(2)}) %all-to-all-start.9) | async-done | bytes 196640 | tf_op jit(solution)/shard_map/all_to_all | solution.py:133
  166.6 0.7 reshape.139
  167.3 6.3 %all-to-all-start.10 = ((f32[8,1,128]{2,1,0:T(1,128)}), f32[8,1,128]{2,1,0:T(1,128)S(1)}, u32[]{:S(2)}, u32[]{:S(2)}) async-start(f32[8,1,128]{2,1,0:T(1,128)} %reshape.139), calls=%async_computation.11 | async-start | bytes 8192 | tf_op jit(solution)/shard_map/all_to_all | solution.py:115
  173.6 0.6 slice_bitcast_fusion.8
  174.2 5.8 %all-to-all-done.10 = f32[8,1,128]{2,1,0:T(1,128)S(1)} async-done(((f32[8,1,128]{2,1,0:T(1,128)}), f32[8,1,128]{2,1,0:T(1,128)S(1)}, u32[]{:S(2)}, u32[]{:S(2)}) %all-to-all-start.10) | async-done | bytes 4128 | tf_op jit(solution)/shard_map/all_to_all | solution.py:115
  180.0 0.6 reduce.4
  180.8 0.8 fusion.33
  (97 shorter events, 2.3 us)
Async XLA Ops:
  7.2 14.3 %copy-start.1 = (bf16[4,256,128]{2,1,0:T(8,128)(2,1)S(1)}, bf16[4,256,128]{2,1,0:T(8,128)(2,1)}, u32[]{:S(2)}) copy-start(bf16[4,256,128]{2,1,0:T(8,128)(2,1)} %param.18) | copy-start | bytes 786436
  7.2 14.1 %copy-start = (bf16[4,256,128]{2,1,0:T(8,128)(2,1)S(1)}, bf16[4,256,128]{2,1,0:T(8,128)(2,1)}, u32[]{:S(2)}) copy-start(bf16[4,256,128]{2,1,0:T(8,128)(2,1)} %param.19) | copy-start | bytes 786436
  7.2 14.0 %copy-start.11 = (bf16[4,256,128]{2,1,0:T(8,128)(2,1)S(1)}, bf16[4,256,128]{2,1,0:T(8,128)(2,1)}, u32[]{:S(2)}) copy-start(bf16[4,256,128]{2,1,0:T(8,128)(2,1)} %param.20) | copy-start | bytes 786436
  7.2 14.2 %copy-start.5 = (bf16[4,256,128]{2,1,0:T(8,128)(2,1)S(1)}, bf16[4,256,128]{2,1,0:T(8,128)(2,1)}, u32[]{:S(2)}) copy-start(bf16[4,256,128]{2,1,0:T(8,128)(2,1)} %param.22) | copy-start | bytes 786436
  11.4 11.8 %all-to-all-start.1 = ((bf16[4,4,64,128]{3,2,1,0:T(8,128)(2,1)}), bf16[4,4,64,128]{3,2,1,0:T(8,128)(2,1)S(1)}, u32[]{:S(2)}, u32[]{:S(2)}) async-start(bf16[4,4,64,128]{3,2,1,0:T(8,128)(2,1)} %pad_maximum_fusion.2), calls=%async_computation.1 | async-start | bytes 524288 | tf_op jit(solution)/shard_map/all_to_all | solution.py:133
  19.0 3.5 %copy-start.20 = (f32[4,64]{1,0:T(4,128)S(1)}, f32[4,64]{1,0:T(4,128)}, u32[]{:S(2)}) copy-start(f32[4,64]{1,0:T(4,128)} %param.30) | copy-start | bytes 3076
  21.5 8.2 %copy-start.12 = (bf16[4,256,128]{2,1,0:T(8,128)(2,1)S(1)}, bf16[4,256,128]{2,1,0:T(8,128)(2,1)}, u32[]{:S(2)}) copy-start(bf16[4,256,128]{2,1,0:T(8,128)(2,1)} %param.21) | copy-start | bytes 786436
  21.5 8.4 %copy-start.19 = (f32[4,256]{1,0:T(4,128)S(1)}, f32[4,256]{1,0:T(4,128)}, u32[]{:S(2)}) copy-start(f32[4,256]{1,0:T(4,128)} %param.23) | copy-start | bytes 12292
  21.5 8.4 %copy-start.3 = (s32[4,2048,32]{1,2,0:T(8,128)S(1)}, s32[4,2048,32]{1,2,0:T(8,128)}, u32[]{:S(2)}) copy-start(s32[4,2048,32]{1,2,0:T(8,128)} %param.31) | copy-start | bytes 3145732
  23.8 11.5 %all-to-all-start = ((f32[8,1,640]{2,1,0:T(1,128)}), f32[8,1,640]{2,1,0:T(1,128)S(1)}, u32[]{:S(2)}, u32[]{:S(2)}) async-start(f32[8,1,640]{2,1,0:T(1,128)} %broadcast_in_dim.8), calls=%async_computation | async-start | bytes 40960 | tf_op jit(solution)/shard_map/all_to_all | solution.py:115
  28.7 2.0 %copy-start.13 = (bf16[4,64,128]{2,1,0:T(8,128)(2,1)S(1)}, bf16[4,64,128]{2,1,0:T(8,128)(2,1)}, u32[]{:S(2)}) copy-start(bf16[4,64,128]{2,1,0:T(8,128)(2,1)} %param.29) | copy-start | bytes 196612
  28.7 2.2 %copy-start.4 = (s32[4,256,256]{2,1,0:T(8,128)S(1)}, s32[4,256,256]{2,1,0:T(8,128)}, u32[]{:S(2)}) copy-start(s32[4,256,256]{2,1,0:T(8,128)} %param.24) | copy-start | bytes 3145732
  28.8 67.5 %all-gather.3.cloned.1.call-start = ((), (), s32[]{:S(2)}) async-start(), calls=%async_computation.13 | async-start | bytes 2359296 | tf_op jit(solution)/shard_map/all_gather | solution.py:176
  29.6 1.2 copy-start.14
  29.9 24.1 %copy-start.15 = (f32[4,128]{1,0:T(4,128)S(1)}, f32[4,128]{1,0:T(4,128)}, u32[]{:S(2)}) copy-start(f32[4,128]{1,0:T(4,128)} %param.32) | copy-start | bytes 6148
  29.9 24.1 %copy-start.16 = (f32[4,128]{1,0:T(4,128)S(1)}, f32[4,128]{1,0:T(4,128)}, u32[]{:S(2)}) copy-start(f32[4,128]{1,0:T(4,128)} %param.35) | copy-start | bytes 6148
  31.0 35.1 %copy-start.17 = (f32[4,128]{1,0:T(4,128)S(1)}, f32[4,128]{1,0:T(4,128)}, u32[]{:S(2)}) copy-start(f32[4,128]{1,0:T(4,128)} %param.33) | copy-start | bytes 6148
  31.0 35.1 %copy-start.18 = (f32[4,128]{1,0:T(4,128)S(1)}, f32[4,128]{1,0:T(4,128)}, u32[]{:S(2)}) copy-start(f32[4,128]{1,0:T(4,128)} %param.34) | copy-start | bytes 6148
  36.0 8.7 %all-to-all-start.4 = ((f32[4,4,256]{2,1,0:T(4,128)}), f32[4,4,256]{2,1,0:T(4,128)S(1)}, u32[]{:S(2)}, u32[]{:S(2)}) async-start(f32[4,4,256]{2,1,0:T(4,128)} %pad_maximum_fusion.5), calls=%async_computation.4 | async-start | bytes 32768 | tf_op jit(solution)/shard_map/all_to_all | solution.py:133
  44.7 17.5 %all-to-all-start.2 = ((f32[32,1,256]{2,1,0:T(1,128)}), f32[32,1,256]{2,1,0:T(1,128)S(1)}, u32[]{:S(2)}, u32[]{:S(2)}) async-start(f32[32,1,256]{2,1,0:T(1,128)} %reshape.137), calls=%async_computation.2 | async-start | bytes 65536 | tf_op jit(solution)/shard_map/all_to_all | solution.py:206
  62.2 17.5 %all-to-all-start.3 = ((bf16[4,4,256,128]{3,2,1,0:T(8,128)(2,1)}), bf16[4,4,256,128]{3,2,1,0:T(8,128)(2,1)S(1)}, u32[]{:S(2)}, u32[]{:S(2)}) async-start(bf16[4,4,256,128]{3,2,1,0:T(8,128)(2,1)} %pad_maximum_fusion), calls=%async_computation.3 | async-start | bytes 2097152 | tf_op jit(solution)/shard_map/all_to_all | solution.py:133
  79.7 12.3 %all-to-all-start.6 = ((s16[4,32,2048]{2,1,0:T(8,128)(2,1)}), s16[4,32,2048]{2,1,0:T(8,128)(2,1)S(1)}, u32[]{:S(2)}, u32[]{:S(2)}) async-start(s16[4,32,2048]{2,1,0:T(8,128)(2,1)} %convert_bitcast_fusion), calls=%async_computation.6 | async-start | bytes 1048576 | tf_op jit(solution)/shard_map/all_to_all | solution.py:133
  92.0 8.3 %copy-start.9 = (s16[4,32,2048]{2,1,0:T(8,128)(2,1)}, s16[4,32,2048]{2,1,0:T(8,128)(2,1)S(1)}, u32[]{:S(2)}) copy-start(s16[4,32,2048]{2,1,0:T(8,128)(2,1)S(1)} %all-to-all-done.6.aud_words) | copy-start | bytes 1572868
  92.0 12.3 %all-to-all-start.5 = ((s16[4,256,256]{2,1,0:T(8,128)(2,1)}), s16[4,256,256]{2,1,0:T(8,128)(2,1)S(1)}, u32[]{:S(2)}, u32[]{:S(2)}) async-start(s16[4,256,256]{2,1,0:T(8,128)(2,1)} %convert_bitcast_fusion.1), calls=%async_computation.5 | async-start | bytes 1048576 | tf_op jit(solution)/shard_map/all_to_all | solution.py:133
  96.3 55.1 %reduce-scatter.2.cloned.1.call-start = ((), (), s32[]{:S(2)}) async-start(), calls=%async_computation.12 | async-start | bytes 1769472 | tf_op jit(solution)/shard_map/reduce_scatter | solution.py:243
  96.3 2.5 %copy-start.2 = (bf16[32,256,128]{2,1,0:T(8,128)(2,1)S(1)}, bf16[32,256,128]{2,1,0:T(8,128)(2,1)}, u32[]{:S(2)}) copy-start(bf16[32,256,128]{2,1,0:T(8,128)(2,1)} %all-gather.3.cloned.1.call-done) | copy-start | bytes 6291460
  104.2 0.8 copy-start.10
  122.1 1.2 copy-start.8
  138.1 28.3 %copy-start.6 = (bf16[4,64,128]{2,1,0:T(8,128)(2,1)S(1)}, bf16[4,64,128]{2,1,0:T(8,128)(2,1)}, u32[]{:S(2)}) copy-start(bf16[4,64,128]{2,1,0:T(8,128)(2,1)} %param.26) | copy-start | bytes 196612
  138.1 28.3 %copy-start.7 = (bf16[4,64,128]{2,1,0:T(8,128)(2,1)S(1)}, bf16[4,64,128]{2,1,0:T(8,128)(2,1)}, u32[]{:S(2)}) copy-start(bf16[4,64,128]{2,1,0:T(8,128)(2,1)} %param.25) | copy-start | bytes 196612
  139.1 9.8 %all-to-all-start.8 = ((f32[8,2,256]{2,1,0:T(2,128)}), f32[8,2,256]{2,1,0:T(2,128)S(1)}, u32[]{:S(2)}, u32[]{:S(2)}) async-start(f32[8,2,256]{2,1,0:T(2,128)} %broadcast_in_dim.10), calls=%async_computation.8 | async-start | bytes 32768 | tf_op jit(solution)/shard_map/all_to_all | solution.py:115
  153.9 12.4 %all-to-all-start.9 = ((bf16[4,3,64,128]{3,2,1,0:T(8,128)(2,1)}), bf16[4,3,64,128]{3,2,1,0:T(8,128)(2,1)S(1)}, u32[]{:S(2)}, u32[]{:S(2)}) async-start(bf16[4,3,64,128]{3,2,1,0:T(8,128)(2,1)} %pad_maximum_fusion.4), calls=%async_computation.10 | async-start | bytes 393216 | tf_op jit(solution)/shard_map/all_to_all | solution.py:133
  167.3 12.8 %all-to-all-start.10 = ((f32[8,1,128]{2,1,0:T(1,128)}), f32[8,1,128]{2,1,0:T(1,128)S(1)}, u32[]{:S(2)}, u32[]{:S(2)}) async-start(f32[8,1,128]{2,1,0:T(1,128)} %reshape.139), calls=%async_computation.11 | async-start | bytes 8192 | tf_op jit(solution)/shard_map/all_to_all | solution.py:115
Sparse Core Ops, SparseCore 0:
  32.0 41.6 all-gather.2
  122.3 29.0 reduce-scatter.1

commit v2 on v1

v2 whole, which is shorter than its diff:
```python
import functools
import math

import jax
import jax.numpy as jnp
from jax import lax
from jax.experimental import pallas as pl
from jax.experimental.pallas import tpu as pltpu
from jax.sharding import Mesh
from jax.sharding import PartitionSpec as P

EPS = 1e-06
LOG2E = math.log2(math.e)
F32 = jnp.float32
BF16 = jnp.bfloat16
PLANES, NEAR, CORES, HEAD_GROUPS = 8, 2, 2, 8
QUAD = NEAR * CORES
LINES = 16
QUAD_AXES = ("near", "core")
CTX_AXES = ("plane", "near", "core")


def dot_nt(left, right):
    return lax.dot_general(left, right, (((1,), (1,)), ((), ())), preferred_element_type=F32)


def dot_nn(left, right):
    return lax.dot_general(left, right, (((1,), (0,)), ((), ())), preferred_element_type=F32)


def dot_tn(left, right):
    return lax.dot_general(left, right, (((0,), (0,)), ((), ())), preferred_element_type=F32)


def keep_rows(words, group):
    wide = words.astype(F32).astype(jnp.int32)
    picked = [
        jnp.bitwise_and(wide[first : first + group], 1 << bit)
        for first in range(0, words.shape[0], group)
        for bit in range(8)
    ]
    return jnp.concatenate(picked, axis=0) != 0


def probs_and_scores(keys, values, queries, twice_grad, lse2, delta, kept, coefficient):
    probs = jnp.exp2(dot_nt(keys, queries) * coefficient - lse2)
    dropped = jnp.where(kept, probs, 0.0).astype(BF16)
    prob_grad = jnp.where(kept, dot_nt(values, twice_grad), 0.0)
    return dropped, (probs * (prob_grad - delta)).astype(BF16)


def attention_kernel(ids, *refs, scale, count, first, last):
    coefficient = scale * LOG2E
    pieces = QUAD
    refs = list(refs)

    def take(number):
        taken, refs[:number] = refs[:number], []
        return taken

    per_plane = [(take(1)[0], take(1)[0], take(pieces), take(pieces)) for _ in range(count)]
    vid_kv, vid_qg, vid_small = take(pieces), take(pieces), take(pieces)
    if not first:
        sums_in, refs = refs[0], refs[1:]
    aud_out, vid_out = refs[:2]
    own = ids[0]
    rows, wide = vid_kv[0].shape
    dim = wide // 2

    def joined(blocks, axis=0):
        return jnp.concatenate([block[...] for block in blocks], axis=axis)

    both = joined(vid_kv)
    k_v, v_v = both[:, :dim], both[:, dim:]
    both = joined(vid_qg)
    q_v, g_v = both[:, :dim], both[:, dim:]
    small = joined(vid_small, 1).astype(F32)
    small = small[0:2] + small[2:4] + small[4:6]
    lse_v, delta_v = small[0:1], small[1:2]
    sums = [jnp.zeros((pieces * rows, dim), F32) if first else sums_in[i] for i in range(3)]
    for i, (aud_kv, aud_qg, words_v, words_a) in enumerate(per_plane):
        k_a, v_a = aud_kv[:rows], aud_kv[rows : 2 * rows]
        q_a, g_a = aud_qg[:rows], aud_qg[rows : 2 * rows]
        small = aud_qg[2 * rows :].astype(F32)
        small = small[0:4] + small[4:8] + small[8:12]
        lse_a, delta_a = [
            jnp.concatenate([small[j : j + 1], small[j + 1 : j + 2]], axis=1) for j in (0, 2)
        ]
        kept = keep_rows(joined(words_v, 1), 8)
        dropped, score_grad = probs_and_scores(
            k_a, v_a, q_v, g_v, lse_v, delta_v, kept, coefficient
        )
        aud_out[i, 0] = dot_nn(score_grad, q_v) * scale
        aud_out[i, 1] = dot_nn(dropped, g_v)
        sums[2] = sums[2] + dot_tn(score_grad, k_a)
        kept = keep_rows(joined(words_a), rows // 8)
        dropped, score_grad = probs_and_scores(
            k_v, v_v, q_a, g_a, lse_a, delta_a, kept, coefficient
        )
        sums[1] = sums[1] + dot_nn(dropped, g_a)
        sums[0] = sums[0] + dot_nn(score_grad, q_a)
        aud_out[i, 2] = dot_tn(score_grad, k_v) * scale
    if last:
        sums = [sums[0] * scale, sums[1], sums[2] * scale]
        for i in range(pieces):
            for j in range(3):
                vid_out[jnp.bitwise_xor(own, i), j] = sums[j][i * rows : (i + 1) * rows].astype(BF16)
    else:
        for j in range(3):
            vid_out[j] = sums[j]


def attention(ids, planes, words, video, sums, last, scale):
    count, first = len(planes), sums is None
    pieces, wide = len(video), video[0].shape[1]
    dim, rows = wide // 2, wide
    plane_words, vid_count = rows // 8, pieces * rows
    specs, operands = [], []

    def add(array, shape, index):
        operands.append(array)
        specs.append(pl.BlockSpec(shape, index))

    for i, halves in enumerate(planes):
        if len(halves) == 1:
            add(halves[0], (2 * rows, dim), lambda c, s: (0, 0))
            add(halves[0], (pl.Element(2 * rows + LINES), pl.Element(dim)), lambda c, s: (2 * rows, 0))
        else:
            for half in halves:
                add(half, half.shape, lambda c, s: (0, 0))
        for piece in video:
            add(piece, (plane_words, wide), lambda c, s, i=i: (2 * rows // plane_words + s[1 + i], 0))
        for piece in words:
            add(piece, (plane_words, wide), lambda c, s, i=i: (s[1 + i], 0))
    for depth, place in ((rows, 0), (rows, 1), (LINES, 3 * rows // LINES)):
        for piece in video:
            add(piece, (depth, wide), lambda c, s, place=place: (place, 0))
    if not first:
        add(sums, sums.shape, lambda c, s: (0, 0, 0))
    if last:
        vid_shape, vid_type = (pieces, 3, rows, dim), BF16
    else:
        vid_shape, vid_type = (3, vid_count, dim), F32
    pairs = 2 * count * rows * vid_count
    return pl.pallas_call(
        functools.partial(attention_kernel, scale=scale, count=count, first=first, last=last),
        grid_spec=pltpu.PrefetchScalarGridSpec(
            num_scalar_prefetch=1,
            grid=(1,),
            in_specs=specs,
            out_specs=[
                pl.BlockSpec((count, 3, rows, dim), lambda c, s: (0, 0, 0, 0)),
                pl.BlockSpec(vid_shape, lambda c, s: (0,) * len(vid_shape)),
            ],
        ),
        out_shape=[
            jax.ShapeDtypeStruct((count, 3, rows, dim), F32),
            jax.ShapeDtypeStruct(vid_shape, vid_type),
        ],
        compiler_params=pltpu.CompilerParams(vmem_limit_bytes=32 * 2**20),
        cost_estimate=pl.CostEstimate(
            flops=10 * pairs * dim, bytes_accessed=4 * 2**20, transcendentals=pairs
        ),
    )(ids, *operands)


def from_heads(lines):
    return lax.all_to_all(lines, "head", 0, 0, tiled=True)


def row_line(values):
    return jnp.sum(values.T, axis=0, keepdims=True)


def columns(line, dim):
    return jnp.broadcast_to(line, (dim, line.shape[1])).T


def sums_kernel(aud_k, aud_q, vid_q, vid_k, out):
    lines = []
    pair = []
    for tokens in (aud_k, aud_q, vid_q, vid_k):
        total = 0.0
        for i in range(tokens.shape[0]):
            values = tokens[i].astype(F32)
            total = total + values * values
        pair.append(total)
    both = jnp.concatenate(pair[:2], axis=0)
    line = jnp.concatenate([row_line(both), row_line(pair[2]), row_line(pair[3])], axis=1)
    out[...] = jnp.broadcast_to(line, out.shape)


def head_sums(aud_k, aud_q, vid_q, vid_k):
    rows = 2 * (aud_k.shape[1] + vid_k.shape[1])
    return pl.pallas_call(
        sums_kernel,
        out_shape=jax.ShapeDtypeStruct((HEAD_GROUPS, rows), F32),
        compiler_params=pltpu.CompilerParams(vmem_limit_bytes=16 * 2**20),
    )(aud_k, aud_q, vid_q, vid_k)


def bit_order(values):
    words = values.shape[0] // 8
    return jnp.swapaxes(values.reshape(words, 8, values.shape[1]), 0, 1).reshape(values.shape)


def word_order(values):
    words = values.shape[0] // 8
    return jnp.swapaxes(values.reshape(8, words, values.shape[1]), 0, 1).reshape(values.shape)


def pack_kernel(sums, aud_k, aud_v, aud_q, aud_g, lines, gain_k, gain_q, out, scales, *, features):
    total = jnp.sum(sums[...], axis=0, keepdims=True)
    line = lax.rsqrt(total / features + EPS)
    scales[...] = line
    heads, rows, dim = aud_k.shape
    column = columns(line[:, : 2 * rows], dim)
    for i in range(heads):
        k = (aud_k[i].astype(F32) * column[:rows] * gain_k[i : i + 1]).astype(BF16)
        out[i, :rows] = bit_order(k.astype(F32)).astype(BF16)
        out[i, rows : 2 * rows] = bit_order(aud_v[i].astype(F32)).astype(BF16)
        out[i, 2 * rows : 3 * rows] = (
            aud_q[i].astype(F32) * column[rows:] * gain_q[i : i + 1]
        ).astype(BF16)
        out[i, 3 * rows : 4 * rows] = (2.0 * aud_g[i].astype(F32)).astype(BF16)
        out[i, 4 * rows :] = lines[i]


def pack_audio(sums, aud_k, aud_v, aud_q, aud_g, lines, gain_k, gain_q, features):
    heads, rows, dim = aud_k.shape
    return pl.pallas_call(
        functools.partial(pack_kernel, features=features),
        out_shape=[
            jax.ShapeDtypeStruct((heads, 4 * rows + LINES, dim), BF16),
            jax.ShapeDtypeStruct((1, sums.shape[1]), F32),
        ],
        compiler_params=pltpu.CompilerParams(vmem_limit_bytes=16 * 2**20),
    )(sums, aud_k, aud_v, aud_q, aud_g, lines, gain_k, gain_q)


def finish_kernel(means, scales, *refs, features):
    (aud_k, aud_q, vid_q, vid_k, up_ak, up_aq, up_vq, up_vk,
     gain_ak, gain_aq, gain_vq, gain_vk, out_ak, out_aq, out_vq, out_vk) = refs
    mean_line = jnp.sum(means[...], axis=0, keepdims=True) / features
    scale_line = scales[...]
    heads, rows, dim = aud_k.shape
    cut = 2 * rows
    more = vid_q.shape[1]
    places = [(0, rows, True), (rows, cut, False), (cut, cut + more, False), (cut + more, cut + 2 * more, True)]
    scale_col = columns(scale_line, dim)
    mean_col = columns(mean_line, dim)
    sets = (
        (aud_k, up_ak, gain_ak, out_ak), (aud_q, up_aq, gain_aq, out_aq),
        (vid_q, up_vq, gain_vq, out_vq), (vid_k, up_vk, gain_vk, out_vk),
    )
    for (tokens, up, gain, out), (first, last, bits) in zip(sets, places):
        scale, mean = scale_col[first:last], mean_col[first:last]
        for i in range(heads):
            upstream = up[i].astype(F32)
            if bits:
                upstream = word_order(upstream)
            weighted = upstream * gain[i : i + 1]
            unit = tokens[i].astype(F32) * scale
            out[i] = (scale * (weighted - unit * mean)).astype(BF16)


def finish(means, scales, tokens, ups, gains, features):
    return pl.pallas_call(
        functools.partial(finish_kernel, features=features),
        out_shape=[jax.ShapeDtypeStruct(t.shape, BF16) for t in tokens],
        compiler_params=pltpu.CompilerParams(vmem_limit_bytes=32 * 2**20),
    )(means, scales, *tokens, *ups, *gains)
def pack_video_kernel(
    own, scales, vid_k, vid_v, vid_q, vid_g, mask, lines, gain_k, gain_q, *outs
):
    heads, rows, dim = vid_k.shape
    first = scales.shape[1] - 2 * rows
    column_q = columns(scales[:, first : first + rows], dim)
    column_k = columns(scales[:, first + rows :], dim)
    for i, out in enumerate(outs):
        head = jnp.bitwise_xor(own[0], i)
        k = (vid_k[head].astype(F32) * column_k * gain_k[pl.ds(head, 1), :]).astype(BF16)
        out[:rows, :dim] = bit_order(k.astype(F32)).astype(BF16)
        out[:rows, dim:] = bit_order(vid_v[head].astype(F32)).astype(BF16)
        out[rows : 2 * rows, :dim] = (
            vid_q[head].astype(F32) * column_q * gain_q[pl.ds(head, 1), :]
        ).astype(BF16)
        out[rows : 2 * rows, dim:] = (2.0 * vid_g[head].astype(F32)).astype(BF16)
        out[2 * rows : 3 * rows] = mask[head].astype(F32).T.astype(BF16)
        out[3 * rows :] = lines[head]


def pack_video(own, scales, vid_k, vid_v, vid_q, vid_g, mask, lines, gain_k, gain_q):
    heads, rows, dim = vid_k.shape
    smem = pl.BlockSpec(memory_space=pltpu.SMEM)
    vmem = pl.BlockSpec(memory_space=pltpu.VMEM)
    return pl.pallas_call(
        pack_video_kernel,
        in_specs=[smem] + [vmem] * 9,
        out_shape=[jax.ShapeDtypeStruct((3 * rows + LINES, 2 * dim), BF16)] * heads,
        compiler_params=pltpu.CompilerParams(vmem_limit_bytes=16 * 2**20),
    )(own, scales, vid_k, vid_v, vid_q, vid_g, mask, lines, gain_k, gain_q)


def pack_words_kernel(own, mask, *outs):
    for i, out in enumerate(outs):
        words = mask[jnp.bitwise_xor(own[0], i)].astype(F32).astype(BF16)
        count, wide = words.shape[0], out.shape[1]
        for j in range(words.shape[1] // wide):
            out[j * count : (j + 1) * count] = words[:, j * wide : (j + 1) * wide]


def pack_words(own, mask, wide):
    heads, count, queries = mask.shape
    return pl.pallas_call(
        pack_words_kernel,
        in_specs=[pl.BlockSpec(memory_space=pltpu.SMEM), pl.BlockSpec(memory_space=pltpu.VMEM)],
        out_shape=[jax.ShapeDtypeStruct((count * queries // wide, wide), BF16)] * heads,
        compiler_params=pltpu.CompilerParams(vmem_limit_bytes=16 * 2**20),
    )(own, mask)


def words_first(rows):
    split = rows.reshape(rows.shape[:-2] + (8, rows.shape[-2] // 8, rows.shape[-1]))
    return jnp.swapaxes(split, -3, -2).reshape(rows.shape)


def to_quad(rows):
    return lax.all_to_all(rows, QUAD_AXES, 0, 0, tiled=True)


def shift(rows, step):
    return lax.ppermute(rows, "plane", [(i, (i + step) % PLANES) for i in range(PLANES)])


def after(value, *others):
    return lax.optimization_barrier((value,) + others)[0]


def token_sums(tokens, scales, gain_rows, upstream):
    weighted = upstream.astype(F32) * gain_rows[:, None, :]
    return jnp.sum(weighted * (tokens.astype(F32) * scales[None, :, None]), axis=(0, 2))


def local(
    vid_query, vid_key, vid_value, vid_out, vid_grad, vid_lse, vid_mask,
    aud_query, aud_key, aud_value, aud_out, aud_grad, aud_lse, aud_mask,
    gain_vq, gain_ak, gain_aq, gain_vk,
):
    heads, vid_rows, dim = vid_query.shape
    aud_rows = aud_query.shape[1]
    plane_rows = QUAD * aud_rows
    feature_count = HEAD_GROUPS * heads * dim
    scale = dim**-0.5
    own_plane = lax.axis_index("plane")
    own = lax.axis_index(QUAD_AXES)

    own_line = own.astype(jnp.int32).reshape(1)

    sums = head_sums(aud_key, aud_query, vid_query, vid_key)
    arrived = from_heads(sums)

    def lines(lse, out, grad):
        delta = jnp.sum(grad.astype(F32) * out.astype(F32), axis=2)
        rest, found = jnp.stack([lse * LOG2E, delta], axis=1), []
        for _ in range(3):
            found.append(lax.reduce_precision(rest, 8, 7))
            rest = rest - found[-1]
        return jnp.stack(found, axis=1).astype(BF16)

    aud_lines = jnp.pad(
        lines(aud_lse, aud_out, aud_grad).reshape(heads, -1, dim),
        ((0, 0), (0, LINES - 6 * aud_rows // dim), (0, 0)),
    )
    vid_lines = jnp.pad(
        lines(vid_lse, vid_out, vid_grad).reshape(heads, 6, vid_rows),
        ((0, 0), (0, LINES - 6), (0, 0)),
    )

    def across_quad(pieces):
        return [pieces[0]] + [
            lax.ppermute(pieces[offset], QUAD_AXES, [(i, i ^ offset) for i in range(QUAD)])
            for offset in range(1, QUAD)
        ]

    words = across_quad(pack_words(after(own_line, sums), jnp.swapaxes(aud_mask, 1, 2), plane_rows))

    audio, scales = pack_audio(
        arrived, aud_key, aud_value, aud_query, aud_grad, aud_lines, gain_ak, gain_aq, feature_count
    )
    video = across_quad(
        pack_video(
            after(own_line, audio), scales, vid_key, vid_value, vid_query, vid_grad, vid_mask,
            vid_lines, gain_vk, gain_vq,
        )
    )
    audio = to_quad(audio)
    mine = audio[:, : 4 * aud_rows].reshape(QUAD, 4, aud_rows, dim).swapaxes(0, 1)
    tail = audio[:, 4 * aud_rows : 4 * aud_rows + 6 * aud_rows // dim].reshape(QUAD, 6, aud_rows)
    tail = tail.swapaxes(0, 1).reshape(6 * plane_rows // dim, dim)
    mine = jnp.concatenate(
        [mine.reshape(4 * plane_rows, dim), jnp.pad(tail, ((0, LINES - tail.shape[0]), (0, 0)))]
    )
    below, above = [mine], [mine]
    for _ in range(3):
        below.append(shift(below[-1], 1))
        above.append(shift(above[-1], -1))
    half = 2 * plane_rows
    far_kv, far_qg = shift(below[-1][:half], 1), shift(above[-1][half:], -1)

    def plane_ids(*offsets):
        return jnp.stack([own.astype(jnp.int32)] + [(own_plane + o) % PLANES for o in offsets]).astype(jnp.int32)

    part_near, total = attention(
        plane_ids(0, -1, 1), [(mine,), (below[1],), (above[1],)], words, video, None, False, scale
    )
    part_2, total = attention(
        plane_ids(-2, 2), [(below[2],), (above[2],)], words, video, total, False, scale
    )
    part_3, total = attention(
        plane_ids(-3, 3), [(below[3],), (above[3],)], words, video, total, False, scale
    )
    down = shift(part_3[0].astype(BF16), -1)
    part_far, vid_parts = attention(
        plane_ids(4), [(far_kv, far_qg)], words, video, total, True, scale
    )
    up = shift(part_far[0].astype(BF16), 1)

    def onward(part, arrived, step):
        return shift((part + arrived.astype(F32)).astype(BF16), step)

    up = onward(part_3[1], up, 1)
    up, down = onward(part_2[1], up, 1), onward(part_2[0], down, -1)
    up, down = onward(part_near[2], up, 1), onward(part_near[1], down, -1)
    aud_parts = (part_near[0] + up.astype(F32) + down.astype(F32)).astype(BF16)

    cuts = (aud_rows, 2 * aud_rows, 2 * aud_rows + vid_rows)
    scale_ak, scale_aq, scale_vq, scale_vk = jnp.split(scales[0], cuts)
    up_vk, grad_vv, up_vq = jnp.swapaxes(to_quad(vid_parts), 0, 1)
    grad_vv = words_first(grad_vv)
    local_vq = token_sums(vid_query, scale_vq, gain_vq, up_vq)
    local_vk = token_sums(vid_key, scale_vk, gain_vk, words_first(up_vk))

    home = aud_parts.reshape(3, QUAD, aud_rows, dim).swapaxes(0, 1)
    up_ak, grad_av, up_aq = jnp.swapaxes(to_quad(home), 0, 1)
    grad_av = words_first(grad_av)
    local_ak = token_sums(aud_key, scale_ak, gain_ak, words_first(up_ak))
    local_aq = token_sums(aud_query, scale_aq, gain_aq, up_aq)

    means = jnp.concatenate([local_ak, local_aq, local_vq, local_vk])
    means = from_heads(jnp.broadcast_to(means[None], (HEAD_GROUPS,) + means.shape))
    grad_ak, grad_aq, grad_vq, grad_vk = finish(
        means, scales, (aud_key, aud_query, vid_query, vid_key), (up_ak, up_aq, up_vq, up_vk),
        (gain_ak, gain_aq, gain_vq, gain_vk), feature_count,
    )
    return grad_vq, grad_vk, grad_vv, grad_aq, grad_ak, grad_av


def solution(mesh):
    fine = Mesh(
        mesh.devices.reshape(PLANES, NEAR, CORES, HEAD_GROUPS), ("plane", "near", "core", "head")
    )
    rows, lines, gain = P("head", CTX_AXES, None), P("head", CTX_AXES), P("head", None)
    return jax.shard_map(
        local,
        mesh=fine,
        in_specs=(rows,) * 5 + (lines, rows) + (rows,) * 5 + (lines, P("head", None, CTX_AXES)) + (gain,) * 4,
        out_specs=(rows,) * 6,
        check_vma=False,
    )
```

time: 190 us -> 141 us (0.74)
  blocking collectives: 14.3 us -> 0 us
  between operations: 14.5 us -> 1.1 us
  other arithmetic: 18.2 us -> 8.17 us
  waiting for transfers between devices: 49.6 us -> 40.3 us
  local copies, waits for them, and re-layouts: 18.1 us -> 12.6 us
  Pallas kernels: 17.1 us -> 22 us
  starting transfers between devices: 56.6 us -> 54.6 us
    ppermute x0 -> x21, starting transfers between devices: none -> 27 us  [the longest x15 21.3 us: shift(): lax.ppermute(rows, 'plane', [(i, (i + step) % PLANES) for i in range(PLAN...]
    ppermute x0 -> x21, waiting for transfers between devices: none -> 24.7 us  [the longest x15 18.1 us: shift(): lax.ppermute(rows, 'plane', [(i, (i + step) % PLANES) for i in range(PLAN...]
    all_to_all x4 -> x2, waiting for transfers between devices: 23.7 us -> 7.28 us  [from_heads(): return lax.all_to_all(lines, 'head', 0, 0, tiled=True)]
    all_to_all x6 -> x3, starting transfers between devices: 32.6 us -> 16.8 us  [to_quad(): return lax.all_to_all(rows, QUAD_AXES, 0, 0, tiled=True)]
    all_to_all x6 -> x3, waiting for transfers between devices: 23.4 us -> 8.27 us  [to_quad(): return lax.all_to_all(rows, QUAD_AXES, 0, 0, tiled=True)]
    all_to_all x1 -> x0, blocking collectives: 14.3 us -> none  [to_quad(): return lax.all_to_all(rows, QUAD_AXES, 0, 0, tiled=True)]
    all_to_all x4 -> x2, starting transfers between devices: 23.9 us -> 10.8 us  [from_heads(): return lax.all_to_all(lines, 'head', 0, 0, tiled=True)]
    pallas_call x1 -> x9, Pallas kernels: 17.1 us -> 22 us  [the longest x4 18 us: attention(): pl.pallas_call(functools.partial(attention_kernel, scale=scale, count=cou...]
  transfers between devices with their start and end apart: 12 -> 26, of which waited for: 11 -> 11; matrix products, arithmetic and copies ran while one was open for 14% -> 7% of each run, Pallas kernels for 0% -> 12%
where the time goes in v2:
time: 141 us; the launch traced here: 139 us
  starting transfers between devices  54.6 us (39%)
  waiting for transfers between devices  40.3 us (29%)
  Pallas kernels  22 us (16%)
  local copies, waits for them, and re-layouts  12.6 us (9%)
  other arithmetic  8.17 us (6%)
    ppermute x15, starting transfers between devices, shift(): lax.ppermute(rows, 'plane', [(i, (i + step) % PLANES) for i in range(PLAN...  21.3 us
    ppermute x15, waiting for transfers between devices, shift(): lax.ppermute(rows, 'plane', [(i, (i + step) % PLANES) for i in range(PLAN...  18.1 us
    pallas_call x4, Pallas kernels, attention(): pl.pallas_call(functools.partial(attention_kernel, scale=scale, count=cou...  18 us
    all_to_all x3, starting transfers between devices, to_quad(): return lax.all_to_all(rows, QUAD_AXES, 0, 0, tiled=True)  16.8 us
    all_to_all x2, starting transfers between devices, from_heads(): return lax.all_to_all(lines, 'head', 0, 0, tiled=True)  10.8 us
    all_to_all x3, waiting for transfers between devices, to_quad(): return lax.all_to_all(rows, QUAD_AXES, 0, 0, tiled=True)  8.27 us
    all_to_all x2, waiting for transfers between devices, from_heads(): return lax.all_to_all(lines, 'head', 0, 0, tiled=True)  7.28 us
    unnamed x52, local copies, waits for them, and re-layouts  7.18 us
  transfers between devices with their start and end apart: 26, of which 11 were waited for; matrix products, arithmetic and copies ran while one was open for 7% of the time, Pallas kernels for 12%

profile of v2, /device:TPU:1, one launch (start us, length us, event | category | flops | bytes accessed | tf_op | source)
XLA Modules:
  0.0 138.7 jit_solution(1590901811847420894)
XLA Ops:
  0.6 0.9 copy-done
  1.6 0.9 copy-done.2
  2.5 0.8 copy-done.9
  3.4 0.8 copy-done.11
  4.3 0.2 shard_map.217
  4.5 0.6 copy.54
  5.1 7.5 %all-to-all-start = ((f32[8,1,640]{2,1,0:T(1,128)}), f32[8,1,640]{2,1,0:T(1,128)S(1)}, u32[]{:S(2)}, u32[]{:S(2)}) async-start(f32[8,1,640]{2,1,0:T(1,128)} %copy.54), calls=%async_computation | async-start | bytes 40960 | tf_op jit(solution)/shard_map/all_to_all | solution.py:168
  12.6 1.2 copy-done.7
  13.9 1.0 collective-permute-start.3
  14.9 0.3 collective-permute-start.4
  15.2 1.4 %collective-permute-start.5 = (bf16[256,256]{1,0:T(8,128)(2,1)S(1)}, bf16[256,256]{1,0:T(8,128)(2,1)S(1)}, u32[]{:S(2)}, u32[]{:S(2)}) collective-permute-start(bf16[256,256]{1,0:T(8,128)(2,1)S(1)} %get-tuple-element.41), channel_id=1, source_target_pairs={{0,24},{8,16},{16,8},{24,0},{1,25},{9,17},{17,9},{25,1},{2,26},{10... | collective-permute-start | bytes 393224 | tf_op jit(solution)/shard_map/ppermute | solution.py:382
  16.7 0.1 multiply_reduce_fusion.3
  16.9 2.2 %all-to-all-done = f32[8,1,640]{2,1,0:T(1,128)S(1)} async-done(((f32[8,1,640]{2,1,0:T(1,128)}), f32[8,1,640]{2,1,0:T(1,128)S(1)}, u32[]{:S(2)}, u32[]{:S(2)}) %all-to-all-start) | async-done | bytes 20512 | tf_op jit(solution)/shard_map/all_to_all | solution.py:168
  19.3 0.9 shard_map.218
  20.1 5.5 %all-to-all-start.1 = ((bf16[4,272,128]{2,1,0:T(8,128)(2,1)}), bf16[4,272,128]{2,1,0:T(8,128)(2,1)S(1)}, u32[]{:S(2)}, u32[]{:S(2)}) async-start(bf16[4,272,128]{2,1,0:T(8,128)(2,1)} %get-tuple-element.30), calls=%async_computation.1 | async-start | bytes 557056 | tf_op jit(solution)/shard_map/all_to_all | solution.py:329
  25.7 5.3 %all-to-all-done.1 = bf16[4,272,128]{2,1,0:T(8,128)(2,1)S(1)} async-done(((bf16[4,272,128]{2,1,0:T(8,128)(2,1)}), bf16[4,272,128]{2,1,0:T(8,128)(2,1)S(1)}, u32[]{:S(2)}, u32[]{:S(2)}) %all-to-all-start.1) | async-done | bytes 278560 | tf_op jit(solution)/shard_map/all_to_all | solution.py:329
  31.2 0.1 reshape.265
  31.3 1.7 %collective-permute-start.6 = (bf16[1040,128]{1,0:T(8,128)(2,1)S(1)}, bf16[1040,128]{1,0:T(8,128)(2,1)S(1)}, u32[]{:S(2)}, u32[]{:S(2)}) collective-permute-start(bf16[1040,128]{1,0:T(8,128)(2,1)S(1)} %fusion.10.refs_0_.refs_1_), channel_id=1, source_target_pairs={{0,32},{32,64},{64,96},{96,128},{128,160},{160,192},{192,224},{224... | collective-permute-start | bytes 798728 | tf_op jit(solution)/shard_map/ppermute | solution.py:333
  33.0 4.0 %collective-permute-start.7 = (bf16[1040,128]{1,0:T(8,128)(2,1)S(1)}, bf16[1040,128]{1,0:T(8,128)(2,1)S(1)}, u32[]{:S(2)}, u32[]{:S(2)}) collective-permute-start(bf16[1040,128]{1,0:T(8,128)(2,1)S(1)} %fusion.10.refs_0_.refs_1_), channel_id=1, source_target_pairs={{0,224},{32,0},{64,32},{96,64},{128,96},{160,128},{192,160},{224,1... | collective-permute-start | bytes 798728 | tf_op jit(solution)/shard_map/ppermute | solution.py:333
  37.0 1.2 multiply_reduce_fusion.1
  38.3 1.2 copy-done.8
  39.6 1.6 %shard_map.219 = (bf16[784,256]{1,0:T(8,128)(2,1)S(1)}, bf16[784,256]{1,0:T(8,128)(2,1)}, bf16[784,256]{1,0:T(8,128)(2,1)}, bf16[784,256]{1,0:T(8,128)(2,1)}) custom-call(s32[1]{0:T(128)} %bitcast.own, f32[1,640]{1,0:T(1,128)S(1)} %get-tuple-element.32.scales, bf16[4,256,128]{2,1,0:T(8,128)(2,1)S(1)} %copy-done.3, bf16[4,256,128]{2,1,0:T(8,128)(2,1)S(1)} %copy-done.14, ...), custom_call_target="tpu_custom_call" | custom-call | tf_op jit(solution)/shard_map/pallas_call | solution.py:297
  41.1 1.2 collective-permute-start
  42.3 0.1 collective-permute-start.1
  42.4 1.6 %collective-permute-start.2 = (bf16[784,256]{1,0:T(8,128)(2,1)}, bf16[784,256]{1,0:T(8,128)(2,1)S(1)}, u32[]{:S(2)}, u32[]{:S(2)}) collective-permute-start(bf16[784,256]{1,0:T(8,128)(2,1)} %get-tuple-element.36), channel_id=1, source_target_pairs={{0,24},{8,16},{16,8},{24,0},{1,25},{9,17},{17,9},{25,1},{2,26},{10... | collective-permute-start | bytes 1204232 | tf_op jit(solution)/shard_map/ppermute | solution.py:382
  44.0 2.7 %collective-permute-start.9 = (bf16[1040,128]{1,0:T(8,128)(2,1)S(1)}, bf16[1040,128]{1,0:T(8,128)(2,1)}, u32[]{:S(2)}, u32[]{:S(2)}) collective-permute-start(bf16[1040,128]{1,0:T(8,128)(2,1)S(1)} %collective-permute-done.7.refs_20_.refs_21_), channel_id=1, source_target_pairs={{0,224},{32,0},{64,32},{96,64},{128,96},{160,128},{192,160},{224,1... | collective-permute-start | bytes 798728 | tf_op jit(solution)/shard_map/ppermute | solution.py:333
  46.9 6.1 %collective-permute-done.8.refs_0_.refs_1_ = bf16[1040,128]{1,0:T(8,128)(2,1)} collective-permute-done((bf16[1040,128]{1,0:T(8,128)(2,1)S(1)}, bf16[1040,128]{1,0:T(8,128)(2,1)}, u32[]{:S(2)}, u32[]{:S(2)}) %collective-permute-start.8) | collective-permute-done | bytes 266272 | tf_op jit(solution)/shard_map/ppermute | solution.py:333
  53.1 2.7 %collective-permute-start.11 = (bf16[1040,128]{1,0:T(8,128)(2,1)}, bf16[1040,128]{1,0:T(8,128)(2,1)S(1)}, u32[]{:S(2)}, u32[]{:S(2)}) collective-permute-start(bf16[1040,128]{1,0:T(8,128)(2,1)} %collective-permute-done.9.refs_10_.refs_11_), channel_id=1, source_target_pairs={{0,224},{32,0},{64,32},{96,64},{128,96},{160,128},{192,160},{224,1... | collective-permute-start | bytes 798728 | tf_op jit(solution)/shard_map/ppermute | solution.py:333
  55.8 6.6 %collective-permute-done.2.refs_5_.refs_15_.refs_25_.refs_33_.refs_37_.refs_41_.refs_23_.refs_27_.refs_31_.refs_13_.refs_17_.refs_21_ = bf16[784,256]{1,0:T(8,128)(2,1)S(1)} collective-permute-done((bf16[784,256]{1,0:T(8,128)(2,1)}, bf16[784,256]{1,0:T(8,128)(2,1)S(1)}, u32[]{:S(2)}, u32[]{:S(2)}) %collective-permute-start.2) | collective-permute-done | bytes 401440 | tf_op jit(solution)/shard_map/ppermute | solution.py:382
  62.4 5.6 %shard_map.221 = (f32[3,3,256,128]{3,2,1,0:T(8,128)S(1)}, f32[3,1024,128]{2,1,0:T(8,128)S(1)}) custom-call(s32[4]{0:T(128)S(1)} %pad_add_fusion.ids, bf16[1040,128]{1,0:T(8,128)(2,1)S(1)} %fusion.10.refs_0_.refs_1_, bf16[1040,128]{1,0:T(8,128)(2,1)S(1)} %fusion.10.refs_0_.refs_1_, ...), custom_call_target="tpu_custom_call" | custom-call | flops 2013265920 | bytes 4194304 | tf_op jit(solution)/shard_map/pallas_call | solution.py:145
  68.1 1.1 copy-done.4
  69.1 1.7 %collective-permute-start.13 = (bf16[528,128]{1,0:T(8,128)(2,1)S(1)}, bf16[528,128]{1,0:T(8,128)(2,1)S(1)}, u32[]{:S(2)}, u32[]{:S(2)}) collective-permute-start(bf16[528,128]{1,0:T(8,128)(2,1)S(1)} %slice.52), channel_id=1, source_target_pairs={{0,224},{32,0},{64,32},{96,64},{128,96},{160,128},{192,160},{224,1... | collective-permute-start | bytes 405512 | tf_op jit(solution)/shard_map/ppermute | solution.py:333
  70.9 0.3 collective-permute-start.12
  71.2 5.1 %shard_map.222 = (f32[2,3,256,128]{3,2,1,0:T(8,128)S(1)}, f32[3,1024,128]{2,1,0:T(8,128)S(1)}) custom-call(s32[3]{0:T(128)S(1)} %pad_add_fusion.1.ids, bf16[1040,128]{1,0:T(8,128)(2,1)} %collective-permute-done.8.refs_0_.refs_1_, bf16[1040,128]{1,0:T(8,128)(2,1)} %collective-permute-done.8.refs_0_.refs_1_, ...), custom_call_target="tpu_custom_call" | custom-call | flops 1342177280 | bytes 4194304 | tf_op jit(solution)/shard_map/pallas_call | solution.py:145
  76.3 4.0 %shard_map.223 = (f32[2,3,256,128]{3,2,1,0:T(8,128)S(1)}, f32[3,1024,128]{2,1,0:T(8,128)S(1)}) custom-call(s32[3]{0:T(128)S(1)} %pad_add_fusion.2.ids, bf16[1040,128]{1,0:T(8,128)(2,1)S(1)} %collective-permute-done.10.refs_0_.refs_1_, bf16[1040,128]{1,0:T(8,128)(2,1)S(1)} %collective-permute-done.10.refs_0_.refs_1_, ...), custom_call_target="tpu_custom_call" | custom-call | flops 1342177280 | bytes 4194304 | tf_op jit(solution)/shard_map/pallas_call | solution.py:145
  80.3 3.3 %shard_map.224 = (f32[1,3,256,128]{3,2,1,0:T(8,128)S(1)}, bf16[4,3,256,128]{3,2,1,0:T(8,128)(2,1)}) custom-call(s32[2]{0:T(128)S(1)} %pad_add_fusion.3.ids, bf16[512,128]{1,0:T(8,128)(2,1)S(1)} %collective-permute-done.12.refs_0_, bf16[528,128]{1,0:T(8,128)(2,1)S(1)} %collective-permute-done.13.refs_1_, ...), custom_call_target="tpu_custom_call" | custom-call | flops 671088640 | bytes 4194304 | tf_op jit(solution)/shard_map/pallas_call | solution.py:145
  83.8 0.7 fusion.11
  84.5 2.7 %collective-permute-start.18 = (bf16[3,256,128]{2,1,0:T(8,128)(2,1)}, bf16[3,256,128]{2,1,0:T(8,128)(2,1)}, u32[]{:S(2)}, u32[]{:S(2)}) collective-permute-start(bf16[3,256,128]{2,1,0:T(8,128)(2,1)} %fusion.11), channel_id=1, source_target_pairs={{0,224},{32,0},{64,32},{96,64},{128,96},{160,128},{192,160},{224,1... | collective-permute-start | bytes 589832 | tf_op jit(solution)/shard_map/ppermute | solution.py:333
  87.1 4.1 %collective-permute-done.14 = bf16[3,256,128]{2,1,0:T(8,128)(2,1)S(1)} collective-permute-done((bf16[3,256,128]{2,1,0:T(8,128)(2,1)S(1)}, bf16[3,256,128]{2,1,0:T(8,128)(2,1)S(1)}, u32[]{:S(2)}, u32[]{:S(2)}) %collective-permute-start.14) | collective-permute-done | bytes 196640 | tf_op jit(solution)/shard_map/ppermute | solution.py:333
  91.2 0.7 fusion.5
  92.0 4.6 %all-to-all-start.3 = ((bf16[4,3,256,128]{3,2,1,0:T(8,128)(2,1)}), bf16[4,3,256,128]{3,2,1,0:T(8,128)(2,1)S(1)}, u32[]{:S(2)}, u32[]{:S(2)}) async-start(bf16[4,3,256,128]{3,2,1,0:T(8,128)(2,1)} %get-tuple-element.49), calls=%async_computation.3 | async-start | bytes 1572864 | tf_op jit(solution)/shard_map/all_to_all | solution.py:329
  96.6 2.2 %collective-permute-done.15 = bf16[3,256,128]{2,1,0:T(8,128)(2,1)} collective-permute-done((bf16[3,256,128]{2,1,0:T(8,128)(2,1)}, bf16[3,256,128]{2,1,0:T(8,128)(2,1)}, u32[]{:S(2)}, u32[]{:S(2)}) %collective-permute-start.15) | collective-permute-done | bytes 196640 | tf_op jit(solution)/shard_map/ppermute | solution.py:333
  98.8 1.1 fusion.6
  100.0 2.7 %collective-permute-start.19 = (bf16[3,256,128]{2,1,0:T(8,128)(2,1)S(1)}, bf16[3,256,128]{2,1,0:T(8,128)(2,1)S(1)}, u32[]{:S(2)}, u32[]{:S(2)}) collective-permute-start(bf16[3,256,128]{2,1,0:T(8,128)(2,1)S(1)} %get-tuple-element.61), channel_id=1, source_target_pairs={{0,224},{32,0},{64,32},{96,64},{128,96},{160,128},{192,160},{224,1... | collective-permute-start | bytes 589832 | tf_op jit(solution)/shard_map/ppermute | solution.py:333
  102.8 3.0 %collective-permute-done.16 = bf16[3,256,128]{2,1,0:T(8,128)(2,1)S(1)} collective-permute-done((bf16[3,256,128]{2,1,0:T(8,128)(2,1)S(1)}, bf16[3,256,128]{2,1,0:T(8,128)(2,1)S(1)}, u32[]{:S(2)}, u32[]{:S(2)}) %collective-permute-start.16) | collective-permute-done | bytes 196640 | tf_op jit(solution)/shard_map/ppermute | solution.py:333
  105.8 0.8 fusion.7
  106.6 2.0 %collective-permute-start.17 = (bf16[3,256,128]{2,1,0:T(8,128)(2,1)}, bf16[3,256,128]{2,1,0:T(8,128)(2,1)}, u32[]{:S(2)}, u32[]{:S(2)}) collective-permute-start(bf16[3,256,128]{2,1,0:T(8,128)(2,1)} %get-tuple-element.54), channel_id=1, source_target_pairs={{0,32},{32,64},{64,96},{96,128},{128,160},{160,192},{192,224},{224... | collective-permute-start | bytes 589832 | tf_op jit(solution)/shard_map/ppermute | solution.py:333
  108.5 0.7 collective-permute-start.20
  109.3 0.9 fusion.23
  110.2 0.9 convert_bitcast_fusion
  111.1 1.6 %collective-permute-done.17 = bf16[3,256,128]{2,1,0:T(8,128)(2,1)} collective-permute-done((bf16[3,256,128]{2,1,0:T(8,128)(2,1)}, bf16[3,256,128]{2,1,0:T(8,128)(2,1)}, u32[]{:S(2)}, u32[]{:S(2)}) %collective-permute-start.17) | collective-permute-done | bytes 196640 | tf_op jit(solution)/shard_map/ppermute | solution.py:333
  112.6 1.1 collective-permute-done.20
  113.7 1.1 fusion.9
  114.8 0.7 copy.80
  115.5 6.7 %all-to-all-start.2 = ((bf16[4,3,64,128]{3,2,1,0:T(8,128)(2,1)}), bf16[4,3,64,128]{3,2,1,0:T(8,128)(2,1)S(1)}, u32[]{:S(2)}, u32[]{:S(2)}) async-start(bf16[4,3,64,128]{3,2,1,0:T(8,128)(2,1)} %bitcast.119), calls=%async_computation.2 | async-start | bytes 393216 | tf_op jit(solution)/shard_map/all_to_all | solution.py:329
  122.2 1.5 %fusion.2 = (f32[256]{0:T(256)S(1)}, f32[256]{0:T(256)S(1)}) fusion(f32[4,32,8,128]{3,1,2,0:T(8,128)} %convert_bitcast_fusion, bf16[4,256,128]{2,1,0:T(8,128)(2,1)S(1)} %copy-done.3, f32[256]{0:T(256)S(1)} %bitcast.143, f32[4,128]{1,0:T(4,128)S(1)} %copy-done.19, f32[256]{0:T(256)S(1)} %bitcast.142, bf16[4,256,128]{2,1,0:T(8,128)(2,1)S(1)} %copy-done.1, ...), kind=kLoop, calls=%fused_computation.6 | loop fusion | flops 1441280 | bytes 1318912 | tf_op jit(solution)/shard_map/reduce_sum | solution.py:342
  123.7 2.9 %all-to-all-done.2 = bf16[4,3,64,128]{3,2,1,0:T(8,128)(2,1)S(1)} async-done(((bf16[4,3,64,128]{3,2,1,0:T(8,128)(2,1)}), bf16[4,3,64,128]{3,2,1,0:T(8,128)(2,1)S(1)}, u32[]{:S(2)}, u32[]{:S(2)}) %all-to-all-start.2) | async-done | bytes 196640 | tf_op jit(solution)/shard_map/all_to_all | solution.py:329
  126.7 0.2 fusion.13
  127.0 0.6 broadcast_in_dim.2
  127.6 3.3 %all-to-all-start.4 = ((f32[8,1,640]{2,1,0:T(1,128)}), f32[8,1,640]{2,1,0:T(1,128)S(1)}, u32[]{:S(2)}, u32[]{:S(2)}) async-start(f32[8,1,640]{2,1,0:T(1,128)} %broadcast_in_dim.2), calls=%async_computation.4 | async-start | bytes 40960 | tf_op jit(solution)/shard_map/all_to_all | solution.py:168
  131.0 0.8 copy.78
  131.8 0.6 copy.81
  132.4 5.0 %all-to-all-done.4 = f32[8,1,640]{2,1,0:T(1,128)S(1)} async-done(((f32[8,1,640]{2,1,0:T(1,128)}), f32[8,1,640]{2,1,0:T(1,128)S(1)}, u32[]{:S(2)}, u32[]{:S(2)}) %all-to-all-start.4) | async-done | bytes 20512 | tf_op jit(solution)/shard_map/all_to_all | solution.py:168
  137.5 1.2 shard_map.225
  (96 shorter events, 1.3 us)
Async XLA Ops:
  0.6 1.0 copy-start
  1.6 0.9 copy-start.2
  2.5 0.8 copy-start.9
  3.4 0.8 copy-start.11
  4.2 12.4 %copy-start.24 = (f32[4,64]{1,0:T(4,128)S(1)}, f32[4,64]{1,0:T(4,128)}, u32[]{:S(2)}) copy-start(f32[4,64]{1,0:T(4,128)} %param.30) | copy-start | bytes 3076
  4.2 12.4 %copy-start.15 = (bf16[4,64,128]{2,1,0:T(8,128)(2,1)S(1)}, bf16[4,64,128]{2,1,0:T(8,128)(2,1)}, u32[]{:S(2)}) copy-start(bf16[4,64,128]{2,1,0:T(8,128)(2,1)} %aud_g.1) | copy-start | bytes 196612
  4.2 12.4 %copy-start.22 = (bf16[4,64,128]{2,1,0:T(8,128)(2,1)S(1)}, bf16[4,64,128]{2,1,0:T(8,128)(2,1)}, u32[]{:S(2)}) copy-start(bf16[4,64,128]{2,1,0:T(8,128)(2,1)} %param.28) | copy-start | bytes 196612
  4.2 14.9 %copy-start.10 = (bf16[4,64,128]{2,1,0:T(8,128)(2,1)S(1)}, bf16[4,64,128]{2,1,0:T(8,128)(2,1)}, u32[]{:S(2)}) copy-start(bf16[4,64,128]{2,1,0:T(8,128)(2,1)} %refs_0_.1) | copy-start | bytes 196612
  4.2 14.9 %copy-start.12 = (bf16[4,64,128]{2,1,0:T(8,128)(2,1)S(1)}, bf16[4,64,128]{2,1,0:T(8,128)(2,1)}, u32[]{:S(2)}) copy-start(bf16[4,64,128]{2,1,0:T(8,128)(2,1)} %refs_1_.1) | copy-start | bytes 196612
  4.2 14.9 %copy-start.16 = (bf16[4,64,128]{2,1,0:T(8,128)(2,1)S(1)}, bf16[4,64,128]{2,1,0:T(8,128)(2,1)}, u32[]{:S(2)}) copy-start(bf16[4,64,128]{2,1,0:T(8,128)(2,1)} %aud_v.1) | copy-start | bytes 196612
  4.2 14.9 %copy-start.17 = (f32[4,128]{1,0:T(4,128)S(1)}, f32[4,128]{1,0:T(4,128)}, u32[]{:S(2)}) copy-start(f32[4,128]{1,0:T(4,128)} %refs_8_.1) | copy-start | bytes 6148
  4.3 14.9 %copy-start.18 = (f32[4,128]{1,0:T(4,128)S(1)}, f32[4,128]{1,0:T(4,128)}, u32[]{:S(2)}) copy-start(f32[4,128]{1,0:T(4,128)} %refs_9_.1) | copy-start | bytes 6148
  4.3 21.4 %copy-start.23 = (f32[4,256]{1,0:T(4,128)S(1)}, f32[4,256]{1,0:T(4,128)}, u32[]{:S(2)}) copy-start(f32[4,256]{1,0:T(4,128)} %param.23) | copy-start | bytes 12292
  5.1 14.1 %all-to-all-start = ((f32[8,1,640]{2,1,0:T(1,128)}), f32[8,1,640]{2,1,0:T(1,128)S(1)}, u32[]{:S(2)}, u32[]{:S(2)}) async-start(f32[8,1,640]{2,1,0:T(1,128)} %copy.54), calls=%async_computation | async-start | bytes 40960 | tf_op jit(solution)/shard_map/all_to_all | solution.py:168
  12.6 1.2 copy-start.7
  13.9 23.2 %copy-start.6 = (bf16[4,256,128]{2,1,0:T(8,128)(2,1)S(1)}, bf16[4,256,128]{2,1,0:T(8,128)(2,1)}, u32[]{:S(2)}) copy-start(bf16[4,256,128]{2,1,0:T(8,128)(2,1)} %vid_g.1) | copy-start | bytes 786436
  13.9 27.3 %collective-permute-start.3 = (bf16[256,256]{1,0:T(8,128)(2,1)S(1)}, bf16[256,256]{1,0:T(8,128)(2,1)S(1)}, u32[]{:S(2)}, u32[]{:S(2)}) collective-permute-start(bf16[256,256]{1,0:T(8,128)(2,1)S(1)} %get-tuple-element.39), channel_id=1, source_target_pairs={{0,8},{8,0},{16,24},{24,16},{1,9},{9,1},{17,25},{25,17},{2,10},{10... | collective-permute-start | bytes 393224 | tf_op jit(solution)/shard_map/ppermute | solution.py:382
  14.9 27.4 %collective-permute-start.4 = (bf16[256,256]{1,0:T(8,128)(2,1)S(1)}, bf16[256,256]{1,0:T(8,128)(2,1)S(1)}, u32[]{:S(2)}, u32[]{:S(2)}) collective-permute-start(bf16[256,256]{1,0:T(8,128)(2,1)S(1)} %get-tuple-element.40), channel_id=1, source_target_pairs={{0,16},{8,24},{16,0},{24,8},{1,17},{9,25},{17,1},{25,9},{2,18},{10... | collective-permute-start | bytes 393224 | tf_op jit(solution)/shard_map/ppermute | solution.py:382
  15.2 27.1 %collective-permute-start.5 = (bf16[256,256]{1,0:T(8,128)(2,1)S(1)}, bf16[256,256]{1,0:T(8,128)(2,1)S(1)}, u32[]{:S(2)}, u32[]{:S(2)}) collective-permute-start(bf16[256,256]{1,0:T(8,128)(2,1)S(1)} %get-tuple-element.41), channel_id=1, source_target_pairs={{0,24},{8,16},{16,8},{24,0},{1,25},{9,17},{17,9},{25,1},{2,26},{10... | collective-permute-start | bytes 393224 | tf_op jit(solution)/shard_map/ppermute | solution.py:382
  19.2 19.1 %copy-start.1 = (bf16[4,256,128]{2,1,0:T(8,128)(2,1)S(1)}, bf16[4,256,128]{2,1,0:T(8,128)(2,1)}, u32[]{:S(2)}) copy-start(bf16[4,256,128]{2,1,0:T(8,128)(2,1)} %refs_2_.1) | copy-start | bytes 786436
  19.2 19.1 %copy-start.3 = (bf16[4,256,128]{2,1,0:T(8,128)(2,1)S(1)}, bf16[4,256,128]{2,1,0:T(8,128)(2,1)}, u32[]{:S(2)}) copy-start(bf16[4,256,128]{2,1,0:T(8,128)(2,1)} %refs_3_.1) | copy-start | bytes 786436
  19.2 19.1 %copy-start.14 = (bf16[4,256,128]{2,1,0:T(8,128)(2,1)S(1)}, bf16[4,256,128]{2,1,0:T(8,128)(2,1)}, u32[]{:S(2)}) copy-start(bf16[4,256,128]{2,1,0:T(8,128)(2,1)} %vid_v.1) | copy-start | bytes 786436
  19.2 19.1 %copy-start.19 = (f32[4,128]{1,0:T(4,128)S(1)}, f32[4,128]{1,0:T(4,128)}, u32[]{:S(2)}) copy-start(f32[4,128]{1,0:T(4,128)} %refs_11_.1) | copy-start | bytes 6148
  19.2 19.1 %copy-start.20 = (f32[4,128]{1,0:T(4,128)S(1)}, f32[4,128]{1,0:T(4,128)}, u32[]{:S(2)}) copy-start(f32[4,128]{1,0:T(4,128)} %refs_10_.1) | copy-start | bytes 6148
  20.1 10.9 %all-to-all-start.1 = ((bf16[4,272,128]{2,1,0:T(8,128)(2,1)}), bf16[4,272,128]{2,1,0:T(8,128)(2,1)S(1)}, u32[]{:S(2)}, u32[]{:S(2)}) async-start(bf16[4,272,128]{2,1,0:T(8,128)(2,1)} %get-tuple-element.30), calls=%async_computation.1 | async-start | bytes 557056 | tf_op jit(solution)/shard_map/all_to_all | solution.py:329
  31.3 12.7 %collective-permute-start.6 = (bf16[1040,128]{1,0:T(8,128)(2,1)S(1)}, bf16[1040,128]{1,0:T(8,128)(2,1)S(1)}, u32[]{:S(2)}, u32[]{:S(2)}) collective-permute-start(bf16[1040,128]{1,0:T(8,128)(2,1)S(1)} %fusion.10.refs_0_.refs_1_), channel_id=1, source_target_pairs={{0,32},{32,64},{64,96},{96,128},{128,160},{160,192},{192,224},{224... | collective-permute-start | bytes 798728 | tf_op jit(solution)/shard_map/ppermute | solution.py:333
  33.0 11.0 %collective-permute-start.7 = (bf16[1040,128]{1,0:T(8,128)(2,1)S(1)}, bf16[1040,128]{1,0:T(8,128)(2,1)S(1)}, u32[]{:S(2)}, u32[]{:S(2)}) collective-permute-start(bf16[1040,128]{1,0:T(8,128)(2,1)S(1)} %fusion.10.refs_0_.refs_1_), channel_id=1, source_target_pairs={{0,224},{32,0},{64,32},{96,64},{128,96},{160,128},{192,160},{224,1... | collective-permute-start | bytes 798728 | tf_op jit(solution)/shard_map/ppermute | solution.py:333
  38.3 1.2 copy-start.8
  41.1 14.7 %collective-permute-start = (bf16[784,256]{1,0:T(8,128)(2,1)}, bf16[784,256]{1,0:T(8,128)(2,1)S(1)}, u32[]{:S(2)}, u32[]{:S(2)}) collective-permute-start(bf16[784,256]{1,0:T(8,128)(2,1)} %get-tuple-element.34), channel_id=1, source_target_pairs={{0,8},{8,0},{16,24},{24,16},{1,9},{9,1},{17,25},{25,17},{2,10},{10... | collective-permute-start | bytes 1204232 | tf_op jit(solution)/shard_map/ppermute | solution.py:382
  42.3 13.6 %collective-permute-start.1 = (bf16[784,256]{1,0:T(8,128)(2,1)}, bf16[784,256]{1,0:T(8,128)(2,1)S(1)}, u32[]{:S(2)}, u32[]{:S(2)}) collective-permute-start(bf16[784,256]{1,0:T(8,128)(2,1)} %get-tuple-element.35), channel_id=1, source_target_pairs={{0,16},{8,24},{16,0},{24,8},{1,17},{9,25},{17,1},{25,9},{2,18},{10... | collective-permute-start | bytes 1204232 | tf_op jit(solution)/shard_map/ppermute | solution.py:382
  42.4 20.0 %collective-permute-start.2 = (bf16[784,256]{1,0:T(8,128)(2,1)}, bf16[784,256]{1,0:T(8,128)(2,1)S(1)}, u32[]{:S(2)}, u32[]{:S(2)}) collective-permute-start(bf16[784,256]{1,0:T(8,128)(2,1)} %get-tuple-element.36), channel_id=1, source_target_pairs={{0,24},{8,16},{16,8},{24,0},{1,25},{9,17},{17,9},{25,1},{2,26},{10... | collective-permute-start | bytes 1204232 | tf_op jit(solution)/shard_map/ppermute | solution.py:382
  44.0 9.1 %collective-permute-start.8 = (bf16[1040,128]{1,0:T(8,128)(2,1)S(1)}, bf16[1040,128]{1,0:T(8,128)(2,1)}, u32[]{:S(2)}, u32[]{:S(2)}) collective-permute-start(bf16[1040,128]{1,0:T(8,128)(2,1)S(1)} %collective-permute-done.6.refs_10_.refs_11_), channel_id=1, source_target_pairs={{0,32},{32,64},{64,96},{96,128},{128,160},{160,192},{192,224},{224... | collective-permute-start | bytes 798728 | tf_op jit(solution)/shard_map/ppermute | solution.py:333
  44.0 9.1 %collective-permute-start.9 = (bf16[1040,128]{1,0:T(8,128)(2,1)S(1)}, bf16[1040,128]{1,0:T(8,128)(2,1)}, u32[]{:S(2)}, u32[]{:S(2)}) collective-permute-start(bf16[1040,128]{1,0:T(8,128)(2,1)S(1)} %collective-permute-done.7.refs_20_.refs_21_), channel_id=1, source_target_pairs={{0,224},{32,0},{64,32},{96,64},{128,96},{160,128},{192,160},{224,1... | collective-permute-start | bytes 798728 | tf_op jit(solution)/shard_map/ppermute | solution.py:333
  53.1 17.8 %collective-permute-start.10 = (bf16[1040,128]{1,0:T(8,128)(2,1)}, bf16[1040,128]{1,0:T(8,128)(2,1)S(1)}, u32[]{:S(2)}, u32[]{:S(2)}) collective-permute-start(bf16[1040,128]{1,0:T(8,128)(2,1)} %collective-permute-done.8.refs_0_.refs_1_), channel_id=1, source_target_pairs={{0,32},{32,64},{64,96},{96,128},{128,160},{160,192},{192,224},{224... | collective-permute-start | bytes 798728 | tf_op jit(solution)/shard_map/ppermute | solution.py:333
  53.1 16.0 %collective-permute-start.11 = (bf16[1040,128]{1,0:T(8,128)(2,1)}, bf16[1040,128]{1,0:T(8,128)(2,1)S(1)}, u32[]{:S(2)}, u32[]{:S(2)}) collective-permute-start(bf16[1040,128]{1,0:T(8,128)(2,1)} %collective-permute-done.9.refs_10_.refs_11_), channel_id=1, source_target_pairs={{0,224},{32,0},{64,32},{96,64},{128,96},{160,128},{192,160},{224,1... | collective-permute-start | bytes 798728 | tf_op jit(solution)/shard_map/ppermute | solution.py:333
  68.0 1.1 copy-start.4
  69.1 11.2 %collective-permute-start.13 = (bf16[528,128]{1,0:T(8,128)(2,1)S(1)}, bf16[528,128]{1,0:T(8,128)(2,1)S(1)}, u32[]{:S(2)}, u32[]{:S(2)}) collective-permute-start(bf16[528,128]{1,0:T(8,128)(2,1)S(1)} %slice.52), channel_id=1, source_target_pairs={{0,224},{32,0},{64,32},{96,64},{128,96},{160,128},{192,160},{224,1... | collective-permute-start | bytes 405512 | tf_op jit(solution)/shard_map/ppermute | solution.py:333
  70.9 9.4 %collective-permute-start.12 = (bf16[512,128]{1,0:T(8,128)(2,1)S(1)}, bf16[512,128]{1,0:T(8,128)(2,1)S(1)}, u32[]{:S(2)}, u32[]{:S(2)}) collective-permute-start(bf16[512,128]{1,0:T(8,128)(2,1)S(1)} %slice.51), channel_id=1, source_target_pairs={{0,32},{32,64},{64,96},{96,128},{128,160},{160,192},{192,224},{224... | collective-permute-start | bytes 393224 | tf_op jit(solution)/shard_map/ppermute | solution.py:333
  83.7 7.6 %collective-permute-start.14 = (bf16[3,256,128]{2,1,0:T(8,128)(2,1)S(1)}, bf16[3,256,128]{2,1,0:T(8,128)(2,1)S(1)}, u32[]{:S(2)}, u32[]{:S(2)}) collective-permute-start(bf16[3,256,128]{2,1,0:T(8,128)(2,1)S(1)} %convert_bitcast_fusion.1), channel_id=1, source_target_pairs={{0,32},{32,64},{64,96},{96,128},{128,160},{160,192},{192,224},{224... | collective-permute-start | bytes 589832 | tf_op jit(solution)/shard_map/ppermute | solution.py:333
  84.5 12.1 %collective-permute-start.18 = (bf16[3,256,128]{2,1,0:T(8,128)(2,1)}, bf16[3,256,128]{2,1,0:T(8,128)(2,1)}, u32[]{:S(2)}, u32[]{:S(2)}) collective-permute-start(bf16[3,256,128]{2,1,0:T(8,128)(2,1)} %fusion.11), channel_id=1, source_target_pairs={{0,224},{32,0},{64,32},{96,64},{128,96},{160,128},{192,160},{224,1... | collective-permute-start | bytes 589832 | tf_op jit(solution)/shard_map/ppermute | solution.py:333
  92.0 6.9 %collective-permute-start.15 = (bf16[3,256,128]{2,1,0:T(8,128)(2,1)}, bf16[3,256,128]{2,1,0:T(8,128)(2,1)}, u32[]{:S(2)}, u32[]{:S(2)}) collective-permute-start(bf16[3,256,128]{2,1,0:T(8,128)(2,1)} %fusion.5), channel_id=1, source_target_pairs={{0,32},{32,64},{64,96},{96,128},{128,160},{160,192},{192,224},{224... | collective-permute-start | bytes 589832 | tf_op jit(solution)/shard_map/ppermute | solution.py:333
  92.0 13.8 %copy-start.5 = (f32[3,3,256,128]{3,2,1,0:T(8,128)S(1)}, f32[3,3,256,128]{3,2,1,0:T(8,128)}, u32[]{:S(2)}) copy-start(f32[3,3,256,128]{3,2,1,0:T(8,128)} %copy-done.4) | copy-start | bytes 3538948
  92.0 17.3 %all-to-all-start.3 = ((bf16[4,3,256,128]{3,2,1,0:T(8,128)(2,1)}), bf16[4,3,256,128]{3,2,1,0:T(8,128)(2,1)S(1)}, u32[]{:S(2)}, u32[]{:S(2)}) async-start(bf16[4,3,256,128]{3,2,1,0:T(8,128)(2,1)} %get-tuple-element.49), calls=%async_computation.3 | async-start | bytes 1572864 | tf_op jit(solution)/shard_map/all_to_all | solution.py:329
  100.0 5.8 %collective-permute-start.16 = (bf16[3,256,128]{2,1,0:T(8,128)(2,1)S(1)}, bf16[3,256,128]{2,1,0:T(8,128)(2,1)S(1)}, u32[]{:S(2)}, u32[]{:S(2)}) collective-permute-start(bf16[3,256,128]{2,1,0:T(8,128)(2,1)S(1)} %get-tuple-element.60), channel_id=1, source_target_pairs={{0,32},{32,64},{64,96},{96,128},{128,160},{160,192},{192,224},{224... | collective-permute-start | bytes 589832 | tf_op jit(solution)/shard_map/ppermute | solution.py:333
  100.0 5.7 %collective-permute-start.19 = (bf16[3,256,128]{2,1,0:T(8,128)(2,1)S(1)}, bf16[3,256,128]{2,1,0:T(8,128)(2,1)S(1)}, u32[]{:S(2)}, u32[]{:S(2)}) collective-permute-start(bf16[3,256,128]{2,1,0:T(8,128)(2,1)S(1)} %get-tuple-element.61), channel_id=1, source_target_pairs={{0,224},{32,0},{64,32},{96,64},{128,96},{160,128},{192,160},{224,1... | collective-permute-start | bytes 589832 | tf_op jit(solution)/shard_map/ppermute | solution.py:333
  106.6 6.0 %collective-permute-start.17 = (bf16[3,256,128]{2,1,0:T(8,128)(2,1)}, bf16[3,256,128]{2,1,0:T(8,128)(2,1)}, u32[]{:S(2)}, u32[]{:S(2)}) collective-permute-start(bf16[3,256,128]{2,1,0:T(8,128)(2,1)} %get-tuple-element.54), channel_id=1, source_target_pairs={{0,32},{32,64},{64,96},{96,128},{128,160},{160,192},{192,224},{224... | collective-permute-start | bytes 589832 | tf_op jit(solution)/shard_map/ppermute | solution.py:333
  108.5 5.2 %collective-permute-start.20 = (bf16[3,256,128]{2,1,0:T(8,128)(2,1)}, bf16[3,256,128]{2,1,0:T(8,128)(2,1)}, u32[]{:S(2)}, u32[]{:S(2)}) collective-permute-start(bf16[3,256,128]{2,1,0:T(8,128)(2,1)} %get-tuple-element.55), channel_id=1, source_target_pairs={{0,224},{32,0},{64,32},{96,64},{128,96},{160,128},{192,160},{224,1... | collective-permute-start | bytes 589832 | tf_op jit(solution)/shard_map/ppermute | solution.py:333
  114.8 11.9 %copy-start.13 = (bf16[4,64,128]{2,1,0:T(8,128)(2,1)S(1)}, bf16[4,64,128]{2,1,0:T(8,128)(2,1)}, u32[]{:S(2)}) copy-start(bf16[4,64,128]{2,1,0:T(8,128)(2,1)} %refs_1_.1) | copy-start | bytes 196612
  115.5 15.4 %copy-start.21 = (bf16[1,4,256,128]{3,2,1,0:T(8,128)(2,1)S(1)}, bf16[1,4,256,128]{3,2,1,0:T(8,128)(2,1)}, u32[]{:S(2)}) copy-start(bf16[1,4,256,128]{3,2,1,0:T(8,128)(2,1)} %get-tuple-element.56) | copy-start | bytes 786436
  115.5 11.1 %all-to-all-start.2 = ((bf16[4,3,64,128]{3,2,1,0:T(8,128)(2,1)}), bf16[4,3,64,128]{3,2,1,0:T(8,128)(2,1)S(1)}, u32[]{:S(2)}, u32[]{:S(2)}) async-start(bf16[4,3,64,128]{3,2,1,0:T(8,128)(2,1)} %bitcast.119), calls=%async_computation.2 | async-start | bytes 393216 | tf_op jit(solution)/shard_map/all_to_all | solution.py:329
  127.6 9.9 %all-to-all-start.4 = ((f32[8,1,640]{2,1,0:T(1,128)}), f32[8,1,640]{2,1,0:T(1,128)S(1)}, u32[]{:S(2)}, u32[]{:S(2)}) async-start(f32[8,1,640]{2,1,0:T(1,128)} %broadcast_in_dim.2), calls=%async_computation.4 | async-start | bytes 40960 | tf_op jit(solution)/shard_map/all_to_all | solution.py:168
